TPU v7x, 256 devices: a whole 4x4x8 slice. The times are simulated.
256 devices in a mesh: blk: 16 (over x_lo, z), beam: 2 (over x_hi), head: 8 (over y, core).
Axes of the slice: x: 4 (x_hi: 2, x_lo: 2; x = x_hi * 2 + x_lo), y: 4, z: 8, core: 2. Of those that a mesh axis runs over, the one named last changes fastest.
Arguments:
- hidden_in: float32 [2, 512, 4096], P(None, 'beam', 'blk'), may hold values from -41 to 41
- norm_gains: float32 [2, 4096], P(None, 'blk'), may hold values from 0.1 to 1.9
- w_qkv: bfloat16 [4096, 3, 4096], P('blk', None, 'head'), may hold values from -0.09375 to 0.09375
- w_self_out: bfloat16 [4096, 4096], P('head', 'blk'), may hold values from -0.09375 to 0.09375
- w_cross_q: bfloat16 [4096, 4096], P('blk', 'head'), may hold values from -0.09375 to 0.09375
- w_cross_out: bfloat16 [4096, 4096], P('head', 'blk'), may hold values from -0.09375 to 0.09375
- pos_bias: float32 [64, 8], P('head'), may hold values from -4 to 4
- self_cache: bfloat16 [2, 2, 256, 6, 4096], P(None, 'beam', 'blk', None, 'head'), may hold values from -300 to 300
- memory: bfloat16 [2, 2048, 4096], P(None, 'blk', 'head'), may hold values from -300 to 300
- parents: int32 [2, 512], replicated, may hold values from 0 to 511, as said below
Outputs:
- hidden_out: float32 [2, 512, 4096], P(None, 'beam', 'blk')
- cache_out: bfloat16 [2, 2, 256, 8, 4096], P(None, 'beam', 'blk', None, 'head')
Inputs may be any that keep to these rules, and one draw needn't show every extreme that they name: In every step each aligned block of 16 rows takes at most 2 of its parents from any one aligned block of 16 rows, and exactly 2 from at least one.
All inputs are finite; a program needn't handle non-finite values.
Results may differ from a plain program's by a relative error of at most 0.022.
Values may be sent and summed in bfloat16 or wider, within the bound.
A program may use at most 128 MiB of HBM per device.

v0:
```python
import jax
import jax.numpy as jnp
from jax import lax
from jax.sharding import PartitionSpec as P

D = 4096
HEAD_DIM = 64


EPS = 1e-06


def combined_all(value, axis, join):
    gathered = jax.tree.map(
        lambda a, kind: lax.all_gather(a.astype(kind), axis),
        value,
        (jnp.bfloat16, jnp.bfloat16, jnp.bfloat16),
    )

    def take(source):
        return jax.tree.map(
            lambda a, own: lax.dynamic_index_in_dim(a, source, 0, False).astype(own.dtype),
            gathered,
            value,
        )

    return lax.fori_loop(
        1, lax.axis_size(axis), lambda source, state: join(state, take(source)), take(0)
    )


def project(states, norm_gain, weight):
    normed = (states * norm_gain).astype(jnp.bfloat16)
    partial_sum = jnp.dot(normed, weight, preferred_element_type=jnp.float32)
    squares = jnp.sum(states * states, axis=1)
    summed, square_sum = lax.psum((partial_sum, squares), "blk")
    inverse_rms = lax.rsqrt(square_sum / D + EPS)
    return (summed * inverse_rms[:, None]).astype(jnp.bfloat16)


def head_total(partial_sum):
    return lax.psum(partial_sum.astype(jnp.bfloat16), "head").astype(jnp.float32)


def routing(parent_list, block_rows, capacity):
    blk_count = lax.axis_size("blk")
    beam_count = lax.axis_size("beam")
    groups = blk_count * beam_count
    blocks = parent_list.reshape(groups, block_rows)
    source_block = blocks // block_rows
    source_dev = source_block % blk_count * beam_count + source_block // blk_count
    local_row = blocks % block_rows
    matching = source_dev[:, :, None] == source_dev[:, None, :]
    ordering = jnp.arange(block_rows, dtype=jnp.int32)
    earlier = ordering[None, :] < ordering[:, None]
    slot_index = jnp.sum((matching & earlier[None]).astype(jnp.int32), axis=2)
    self_index = lax.axis_index("blk") * beam_count + lax.axis_index("beam")
    owned_rows = source_dev == self_index
    selected = owned_rows[:, :, None] & (
        slot_index[:, :, None] == jnp.arange(capacity, dtype=jnp.int32)[None, None, :]
    )
    send_rows = jnp.sum(selected.astype(jnp.int32) * local_row[:, :, None], axis=1)
    send_rows = (
        send_rows.reshape(beam_count, blk_count, capacity)
        .transpose(1, 0, 2)
        .reshape(groups * capacity)
    )
    own_block = lax.axis_index("beam") * blk_count + lax.axis_index("blk")
    own_source = lax.dynamic_index_in_dim(source_dev, own_block, 0, keepdims=False)
    own_slot = lax.dynamic_index_in_dim(slot_index, own_block, 0, keepdims=False)
    return (send_rows, own_source * capacity + own_slot)


def reorder(cache_block, parent_list, capacity):
    send_rows, recv_rows = routing(parent_list, cache_block.shape[1], capacity)
    outgoing = jnp.take(cache_block, send_rows, axis=1)
    arrived = lax.all_to_all(outgoing, ("blk", "beam"), split_axis=1, concat_axis=1, tiled=True)
    return jnp.take(arrived, recv_rows, axis=1)


def self_attend(queries, grown_cache, position_bias):
    rows_here = grown_cache.shape[1]
    length = grown_cache.shape[2]
    heads_here = position_bias.shape[0]
    split_queries = queries.reshape(rows_here, heads_here, HEAD_DIM)
    key_part = grown_cache[0].reshape(rows_here, length, heads_here, HEAD_DIM)
    value_part = grown_cache[1].reshape(rows_here, length, heads_here, HEAD_DIM)
    scores = (
        jnp.einsum("rhd,rjhd->rhj", split_queries, key_part, preferred_element_type=jnp.float32)
        * HEAD_DIM ** (-0.5)
        + position_bias[None]
    )
    maxima = jnp.max(scores, axis=2, keepdims=True)
    weights = jnp.exp(scores - maxima)
    totals = jnp.sum(weights, axis=2)
    mixed = jnp.einsum(
        "rhj,rjhd->rhd",
        weights.astype(jnp.bfloat16),
        value_part,
        preferred_element_type=jnp.float32,
    )
    mixed = mixed / totals[:, :, None]
    return mixed.reshape(rows_here, heads_here * HEAD_DIM).astype(jnp.bfloat16)


def cross_block(queries, memory):
    rows_here = queries.shape[0]
    heads_here = queries.shape[1] // HEAD_DIM
    split_queries = queries.reshape(rows_here, heads_here, HEAD_DIM)
    key_part = memory[0].reshape(-1, heads_here, HEAD_DIM)
    value_part = memory[1].reshape(-1, heads_here, HEAD_DIM)
    scores = jnp.einsum(
        "rhd,ehd->rhe", split_queries, key_part, preferred_element_type=jnp.float32
    ) * HEAD_DIM ** (-0.5)
    maxima = jnp.max(scores, axis=2)
    weights = jnp.exp(scores - maxima[:, :, None])
    totals = jnp.sum(weights, axis=2)
    accumulated = jnp.einsum(
        "rhe,ehd->rhd", weights.astype(jnp.bfloat16), value_part, preferred_element_type=jnp.float32
    )
    return (accumulated.reshape(rows_here, heads_here * HEAD_DIM), maxima, totals)


def cross_partial(queries, memory):
    rows_here = queries.shape[0]
    blocked = queries.reshape(rows_here // rows_here, rows_here, queries.shape[1])

    def one_block(query_block):
        return cross_block(query_block, memory)

    accumulated, maxima, totals = lax.map(one_block, blocked)
    return (
        accumulated.reshape(rows_here, -1),
        maxima.reshape(rows_here, -1),
        totals.reshape(rows_here, -1),
    )


def combine_parts(earlier_part, later_part):
    accum_first, peak_first, total_first = earlier_part
    accum_second, peak_second, total_second = later_part
    joint_max = jnp.maximum(peak_first, peak_second)
    factor_first = jnp.exp(peak_first - joint_max)
    factor_second = jnp.exp(peak_second - joint_max)
    rows_here, heads_here = peak_first.shape
    scaled_first = accum_first.reshape(rows_here, heads_here, -1) * factor_first[:, :, None]
    scaled_second = accum_second.reshape(rows_here, heads_here, -1) * factor_second[:, :, None]
    joined = (scaled_first + scaled_second).reshape(accum_first.shape)
    return (joined, joint_max, total_first * factor_first + total_second * factor_second)


def body(
    hidden_in,
    norm_gains,
    w_qkv,
    w_self_out,
    w_cross_q,
    w_cross_out,
    pos_bias,
    self_cache,
    memory,
    parents,
):
    blk_count = lax.axis_size("blk")
    beam_count = lax.axis_size("beam")
    block_rows = self_cache.shape[2]
    capacity = max(2, -(-block_rows // (blk_count * beam_count)))
    united_qkv = w_qkv.reshape(w_qkv.shape[0], -1)
    inner_here = w_cross_q.shape[1]
    first_row = lax.axis_index("blk") * block_rows
    steps_total = hidden_in.shape[0]
    held_cache = reorder(self_cache[:, 0], parents[0], capacity)
    outputs = []
    for step_index in range(steps_total):
        following = step_index + 1 < steps_total
        states = hidden_in[step_index]
        fresh_qkv = project(states, norm_gains[0], united_qkv)
        own_qkv = lax.dynamic_slice_in_dim(fresh_qkv, first_row, block_rows, 0).reshape(
            block_rows, 3, inner_here
        )
        fresh_entry = jnp.stack([own_qkv[:, 1], own_qkv[:, 2]])[:, :, None]
        grown_cache = jnp.concatenate([held_cache, fresh_entry], axis=2)
        length = grown_cache.shape[2]
        position_bias = jnp.flip(pos_bias[:, :length], axis=1)
        attended = self_attend(own_qkv[:, 0], grown_cache, position_bias)
        projected = jnp.dot(
            lax.all_gather(attended, "blk", axis=0, tiled=True),
            w_self_out,
            preferred_element_type=jnp.float32,
        )
        middle = states + head_total(projected)
        cross_query = project(middle, norm_gains[1], w_cross_q)
        accumulated, peak_scores, totals = cross_partial(cross_query, memory)
        accumulated, peak_scores, totals = combined_all(
            (accumulated, peak_scores, totals), "blk", combine_parts
        )
        rows_here, heads_here = totals.shape
        cross_mixed = (
            (accumulated.reshape(rows_here, heads_here, -1) / totals[:, :, None])
            .reshape(rows_here, -1)
            .astype(jnp.bfloat16)
        )
        outputs.append(
            middle
            + head_total(jnp.dot(cross_mixed, w_cross_out, preferred_element_type=jnp.float32))
        )
        if following:
            held_cache = reorder(grown_cache, parents[step_index + 1], capacity)
        else:
            held_cache = grown_cache
    return (jnp.stack(outputs), held_cache[:, None])


def solution(mesh):
    placed = (
        P(None, "beam", "blk"),
        P(None, "blk"),
        P("blk", None, "head"),
        P("head", "blk"),
        P("blk", "head"),
        P("head", "blk"),
        P("head", None),
        P(None, "beam", "blk", None, "head"),
        P(None, "blk", "head"),
        P(),
    )
    return jax.shard_map(
        body,
        mesh=mesh,
        in_specs=placed,
        out_specs=(P(None, "beam", "blk"), P(None, "beam", "blk", None, "head")),
        check_vma=False,
    )
```

profile of v0, /device:TPU:1, one launch (start us, length us, event | category | flops | bytes accessed | tf_op | source)
XLA Modules:
  0.0 718.7 jit_solution(7970170962780751000)
XLA Ops:
  8.0 1.4 copy.138
  9.4 1.5 fusion.42
  11.0 1.6 fusion.38
  14.8 2.1 gather_fusion
  16.9 1.7 fusion.16
  18.6 11.9 %all-to-all-start = ((bf16[2,64,6,512]{3,0,2,1:T(2,128)(2,1)}), bf16[2,64,6,512]{3,0,2,1:T(2,128)(2,1)S(1)}, u32[]{:S(2)}, u32[]{:S(2)}) async-start(bf16[2,64,6,512]{3,0,2,1:T(2,128)(2,1)} %fusion.16), calls=%async_computation | async-start | bytes 1572864 | tf_op jit(solution)/shard_map/all_to_all | solution.py:77
  30.8 48.7 %all-reduce.1 = (f32[256]{0:T(256)S(1)}, f32[256]{0:T(256)S(1)}) all-reduce(f32[256]{0:T(256)S(1)} %get-tuple-element.453, f32[256]{0:T(256)S(1)} %get-tuple-element.452), channel_id=1, replica_groups=mesh['blk'=16,'beam'=2,'head'=8] {'blk'}, use_global_device_ids=true, to_apply=%region_18.19 | all-reduce | flops 512 | bytes 4096 | tf_op jit(solution)/shard_map/psum | solution.py:36
  81.4 85.1 %all-reduce.13.cloned.1.call-done = (f32[256,1536]{1,0:T(8,128)}, f32[256,1536]{1,0:T(8,128)}) async-done(((f32[256,1536]{1,0:T(8,128)}, f32[256,1536]{1,0:T(8,128)}), (f32[256,1536]{1,0:T(8,128)}, f32[256,1536]{1,0:T(8,128)})) %all-reduce.13.cloned.1.call-update) | async-done | bytes 3145744 | tf_op jit(solution)/shard_map/psum | solution.py:36
  166.5 1.0 fusion.49
  168.1 2.4 gather_fusion.2
  170.5 1.9 fusion.15
  172.4 5.5 all-to-all-start.1
  178.9 1.1 maximum_reduce_fusion.2
  181.5 33.7 %all_gather.30 = bf16[256,512]{1,0:T(8,128)(2,1)S(1)} all-gather(bf16[16,512]{1,0:T(8,128)(2,1)S(1)} %convert_element_type.302), channel_id=1, replica_groups=mesh['blk'=16,'beam'=2,'head'=8] {'blk'}, dimensions={0}, use_global_device_ids=true | all-gather | bytes 278528 | tf_op jit(solution)/shard_map/all_gather | solution.py:187
  216.1 1.0 gather_fusion.3
  217.5 1.2 maximum_reduce_fusion
  220.8 23.9 %all_gather.34 = bf16[256,512]{1,0:T(8,128)(2,1)S(1)} all-gather(bf16[16,512]{1,0:T(8,128)(2,1)S(1)} %convert_element_type.330), channel_id=1, replica_groups=mesh['blk'=16,'beam'=2,'head'=8] {'blk'}, dimensions={0}, use_global_device_ids=true | all-gather | bytes 278528 | tf_op jit(solution)/shard_map/all_gather | solution.py:187
  245.7 81.4 %all-reduce.17.cloned.1.call-done = (bf16[256,256]{1,0:T(8,128)(2,1)}, bf16[256,256]{1,0:T(8,128)(2,1)}) async-done(((bf16[256,256]{1,0:T(8,128)(2,1)}, bf16[256,256]{1,0:T(8,128)(2,1)}), (bf16[256,256]{1,0:T(8,128)(2,1)}, bf16[256,256]{1,0:T(8,128)(2,1)})) %all-reduce.17.cloned.1.call-update) | async-done | bytes 262160 | tf_op jit(solution)/shard_map/psum | solution.py:42
  327.2 2.0 fusion.44
  329.2 2.0 fusion.40
  331.7 27.8 %all-reduce = (f32[256]{0:T(256)S(1)}, f32[256]{0:T(256)S(1)}) all-reduce(f32[256]{0:T(256)S(1)} %get-tuple-element.451, f32[256]{0:T(256)S(1)} %get-tuple-element.450), channel_id=1, replica_groups=mesh['blk'=16,'beam'=2,'head'=8] {'blk'}, use_global_device_ids=true, to_apply=%region_26.27 | all-reduce | flops 512 | bytes 4096 | tf_op jit(solution)/shard_map/psum | solution.py:36
  359.6 100.0 %all-reduce.11.cloned.1.call-done = (f32[256,512]{1,0:T(8,128)}, f32[256,512]{1,0:T(8,128)}) async-done(((f32[256,512]{1,0:T(8,128)}, f32[256,512]{1,0:T(8,128)}), (f32[256,512]{1,0:T(8,128)}, f32[256,512]{1,0:T(8,128)})) %all-reduce.11.cloned.1.call-update) | async-done | bytes 1048592 | tf_op jit(solution)/shard_map/psum | solution.py:36
  459.5 1.1 multiply_convert_fusion.1
  464.3 26.1 %all-gather = bf16[4096,8]{0,1:T(8,128)(2,1)S(1)} all-gather(bf16[256,8]{0,1:T(8,128)(2,1)S(1)} %convert_element_type.313), channel_id=2, replica_groups=mesh['blk'=16,'beam'=2,'head'=8] {'blk'}, dimensions={0}, use_global_device_ids=true | all-gather | bytes 69632 | tf_op jit(solution)/shard_map/all_gather | solution.py:15
  490.6 24.7 %all-gather.1 = bf16[4096,8]{0,1:T(8,128)(2,1)S(1)} all-gather(bf16[256,8]{0,1:T(8,128)(2,1)S(1)} %fusion.11), channel_id=3, replica_groups=mesh['blk'=16,'beam'=2,'head'=8] {'blk'}, dimensions={0}, use_global_device_ids=true | all-gather | bytes 69632 | tf_op jit(solution)/shard_map/all_gather | solution.py:15
  515.3 25.2 %all-gather.2 = bf16[4096,8]{0,1:T(8,128)(2,1)S(1)} all-gather(bf16[256,8]{0,1:T(8,128)(2,1)S(1)} %convert_element_type.341), channel_id=4, replica_groups=mesh['blk'=16,'beam'=2,'head'=8] {'blk'}, dimensions={0}, use_global_device_ids=true | all-gather | bytes 69632 | tf_op jit(solution)/shard_map/all_gather | solution.py:15
  540.7 25.3 %all-gather.3 = bf16[4096,8]{0,1:T(8,128)(2,1)S(1)} all-gather(bf16[256,8]{0,1:T(8,128)(2,1)S(1)} %fusion.13), channel_id=5, replica_groups=mesh['blk'=16,'beam'=2,'head'=8] {'blk'}, dimensions={0}, use_global_device_ids=true | all-gather | bytes 69632 | tf_op jit(solution)/shard_map/all_gather | solution.py:15
  566.1 1.0 fusion.24
  567.3 21.4 %while.24 = (s32[]{:T(128)}, f32[256,512]{0,1:T(8,128)S(1)}, f32[256,8]{0,1:T(8,128)S(1)}, f32[256,8]{0,1:T(8,128)S(1)}, bf16[16,256,8]{1,2,0:T(8,128)(2,1)S(1)}...) while((s32[]{:T(128)}, f32[256,512]{0,1:T(8,128)S(1)}, ...), condition=%wide.region_14.15_spmd, body=%wide.region_13.14_spmd.sunk | while | flops 540677 | bytes 2433167 | solution.py:27
  567.3 1.0 constant_dynamic-slice_fusion.4
  568.8 1.0 constant_dynamic-slice_fusion.4
  570.2 1.0 constant_dynamic-slice_fusion.4
  571.6 1.0 constant_dynamic-slice_fusion.4
  573.1 1.0 constant_dynamic-slice_fusion.4
  574.5 1.0 constant_dynamic-slice_fusion.4
  575.9 1.0 constant_dynamic-slice_fusion.4
  577.3 1.0 constant_dynamic-slice_fusion.4
  578.8 1.0 constant_dynamic-slice_fusion.4
  580.2 1.0 constant_dynamic-slice_fusion.4
  581.6 1.0 constant_dynamic-slice_fusion.4
  583.1 1.0 constant_dynamic-slice_fusion.4
  584.5 1.0 constant_dynamic-slice_fusion.4
  585.9 1.0 constant_dynamic-slice_fusion.4
  587.3 1.0 constant_dynamic-slice_fusion.4
  588.7 27.0 %all-gather.9.cloned.1.call-done = bf16[16,256,512]{2,1,0:T(8,128)(2,1)} async-done(((bf16[1,256,512]{2,1,0:T(8,128)(2,1)}), bf16[16,256,512]{2,1,0:T(8,128)(2,1)}) %all-gather.9.cloned.1.call-update) | async-done | bytes 4194320 | tf_op jit(solution)/shard_map/all_gather | solution.py:15
  615.7 1.0 fusion.23
  617.0 21.4 %while.25 = (s32[]{:T(128)}, f32[256,512]{0,1:T(8,128)S(1)}, f32[256,8]{0,1:T(8,128)S(1)}, f32[256,8]{0,1:T(8,128)S(1)}, bf16[16,256,8]{1,2,0:T(8,128)(2,1)S(1)}...) while((s32[]{:T(128)}, f32[256,512]{0,1:T(8,128)S(1)}, ...), condition=%wide.region_30.31_spmd, body=%wide.region_29.30_spmd.sunk | while | flops 540677 | bytes 2433167 | solution.py:27
  617.0 1.0 constant_dynamic-slice_fusion.5
  618.5 1.0 constant_dynamic-slice_fusion.5
  619.9 1.0 constant_dynamic-slice_fusion.5
  621.3 1.0 constant_dynamic-slice_fusion.5
  622.7 1.0 constant_dynamic-slice_fusion.5
  624.2 1.0 constant_dynamic-slice_fusion.5
  625.6 1.0 constant_dynamic-slice_fusion.5
  627.0 1.0 constant_dynamic-slice_fusion.5
  628.5 1.0 constant_dynamic-slice_fusion.5
  629.9 1.0 constant_dynamic-slice_fusion.5
  631.3 1.0 constant_dynamic-slice_fusion.5
  632.7 1.0 constant_dynamic-slice_fusion.5
  634.2 1.0 constant_dynamic-slice_fusion.5
  635.6 1.0 constant_dynamic-slice_fusion.5
  637.0 1.0 constant_dynamic-slice_fusion.5
  641.5 68.4 %all-reduce.15.cloned.1.call-done = (bf16[256,256]{1,0:T(8,128)(2,1)}, bf16[256,256]{1,0:T(8,128)(2,1)}) async-done(((bf16[256,256]{1,0:T(8,128)(2,1)}, bf16[256,256]{1,0:T(8,128)(2,1)}), (bf16[256,256]{1,0:T(8,128)(2,1)}, bf16[256,256]{1,0:T(8,128)(2,1)})) %all-reduce.15.cloned.1.call-update) | async-done | bytes 262160 | tf_op jit(solution)/shard_map/psum | solution.py:42
  710.0 1.0 add_bitcast_fusion.1
  (252 shorter events, 33.4 us)
Async XLA Ops:
  7.2 320.0 %copy-start = (bf16[256,512]{1,0:T(8,128)(2,1)S(1)}, bf16[256,512]{1,0:T(8,128)(2,1)}, u32[]{:S(2)}) copy-start(bf16[256,512]{1,0:T(8,128)(2,1)} %param.18) | copy-start | bytes 786436
  7.2 2.2 copy-start.1
  7.2 159.3 %all-reduce.13.cloned.1.call-start = ((), (), s32[]{:S(2)}) async-start(), calls=%async_computation.5 | async-start | bytes 6291456 | tf_op jit(solution)/shard_map/psum | solution.py:36
  12.5 0.7 copy-start.15
  12.5 2.0 copy-start.13
  18.6 61.5 %all-to-all-start = ((bf16[2,64,6,512]{3,0,2,1:T(2,128)(2,1)}), bf16[2,64,6,512]{3,0,2,1:T(2,128)(2,1)S(1)}, u32[]{:S(2)}, u32[]{:S(2)}) async-start(bf16[2,64,6,512]{3,0,2,1:T(2,128)(2,1)} %fusion.16), calls=%async_computation | async-start | bytes 1572864 | tf_op jit(solution)/shard_map/all_to_all | solution.py:77
  170.5 7.6 %copy-start.14 = (f32[8,8]{1,0:T(8,128)S(1)}, f32[8,8]{1,0:T(8,128)}, u32[]{:S(2)}) copy-start(f32[8,8]{1,0:T(8,128)} %param.20) | copy-start | bytes 772
  172.4 43.7 %all-to-all-start.1 = ((bf16[2,64,7,512]{3,0,2,1:T(2,128)(2,1)}), bf16[2,64,7,512]{3,0,2,1:T(2,128)(2,1)S(1)}, u32[]{:S(2)}, u32[]{:S(2)}) async-start(bf16[2,64,7,512]{3,0,2,1:T(2,128)(2,1)} %fusion.15), calls=%async_computation.1 | async-start | bytes 1835008 | tf_op jit(solution)/shard_map/all_to_all | solution.py:77
  177.9 149.3 %all-reduce.17.cloned.1.call-start = ((), (), s32[]{:S(2)}) async-start(), calls=%async_computation.7 | async-start | bytes 524288 | tf_op jit(solution)/shard_map/psum | solution.py:42
  178.6 36.7 %copy-start.7 = (bf16[512,256]{1,0:T(8,128)(2,1)S(1)}, bf16[512,256]{1,0:T(8,128)(2,1)}, u32[]{:S(2)}) copy-start(bf16[512,256]{1,0:T(8,128)(2,1)} %param.17) | copy-start | bytes 786436
  178.6 38.8 %copy-start.10 = (bf16[2,16,1,512]{3,0,2,1:T(2,128)(2,1)}, bf16[2,16,1,512]{3,0,2,1:T(2,128)(2,1)S(1)}, u32[]{:S(2)}) copy-start(bf16[2,16,1,512]{3,0,2,1:T(2,128)(2,1)S(1)} %copy.165) | copy-start | bytes 98308
  217.4 28.2 %copy-start.2 = (bf16[2,16,7,512]{3,0,2,1:T(2,128)(2,1)}, bf16[2,16,7,512]{3,0,2,1:T(2,128)(2,1)S(1)}, u32[]{:S(2)}) copy-start(bf16[2,16,7,512]{3,0,2,1:T(2,128)(2,1)S(1)} %fusion.35) | copy-start | bytes 688132
  245.7 213.8 %all-reduce.11.cloned.1.call-start = ((), (), s32[]{:S(2)}) async-start(), calls=%async_computation.4 | async-start | bytes 2097152 | tf_op jit(solution)/shard_map/psum | solution.py:36
  327.2 4.1 copy-start.12
  329.2 2.4 copy-start.4
  329.2 2.4 copy-start.5
  331.2 234.8 %all-gather.7.cloned.1.call-start = ((), (), s32[]{:S(2)}) async-start(), calls=%async_computation.2 | async-start | bytes 4456448 | tf_op jit(solution)/shard_map/all_gather | solution.py:15
  460.8 1.6 copy-start.9
  462.4 153.3 %all-gather.9.cloned.1.call-start = ((), (), s32[]{:S(2)}) async-start(), calls=%async_computation.3 | async-start | bytes 4456448 | tf_op jit(solution)/shard_map/all_gather | solution.py:15
  464.3 245.7 %all-reduce.15.cloned.1.call-start = ((), (), s32[]{:S(2)}) async-start(), calls=%async_computation.6 | async-start | bytes 524288 | tf_op jit(solution)/shard_map/psum | solution.py:42
  616.9 21.5 %copy-start.8 = (bf16[512,256]{1,0:T(8,128)(2,1)S(1)}, bf16[512,256]{1,0:T(8,128)(2,1)}, u32[]{:S(2)}) copy-start(bf16[512,256]{1,0:T(8,128)(2,1)} %param.19) | copy-start | bytes 786436
  638.4 2.0 copy-start.3
  638.4 2.0 copy-start.11
  638.5 71.5 %copy-start.6 = (bf16[256,256]{1,0:T(8,128)(2,1)S(1)}, bf16[256,256]{1,0:T(8,128)(2,1)}, u32[]{:S(2)}) copy-start(bf16[256,256]{1,0:T(8,128)(2,1)} %get-tuple-element.501) | copy-start | bytes 393220
Sparse Core Ops, SparseCore 0:
  12.7 153.7 all-reduce.12
  245.8 81.3 all-reduce.16
  331.3 128.1 all-reduce.10
  462.5 76.3 all-gather.6
  541.1 74.5 all-gather.8
  640.6 69.3 all-reduce.14
where the time goes:
time: 721 us; the launch traced here: 719 us
  waiting for transfers between devices  362 us (50%)
  blocking collectives  236 us (33%)
  local copies, waits for them, and re-layouts  49.8 us (7%)
  other arithmetic  24.3 us (3%)
  starting transfers between devices  17.8 us (2%)
  between operations  14.9 us (2%)
  matrix products  13.2 us (2%)
    psum x2, waiting for transfers between devices, project(): summed, square_sum = lax.psum((partial_sum, squares), 'blk')  185 us
    psum x2, waiting for transfers between devices, head_total(): lax.psum(partial_sum.astype(jnp.bfloat16), 'head').astype(jnp.float32)  150 us
    all_gather x4, blocking collectives, combined_all(): lax.all_gather(a.astype(kind), axis)  101 us
    psum x2, blocking collectives, project(): summed, square_sum = lax.psum((partial_sum, squares), 'blk')  76.6 us
    all_gather x2, blocking collectives, body(): lax.all_gather(attended, 'blk', axis=0, tiled=True)  57.7 us
    dynamic_slice x60, local copies, waits for them, and re-layouts, take(): lax.dynamic_index_in_dim(a, source, 0, False).astype(own.dtype)  33.3 us
    all_gather x2, waiting for transfers between devices, combined_all(): lax.all_gather(a.astype(kind), axis)  27 us
    all_to_all x2, starting transfers between devices, reorder(): lax.all_to_all(outgoing, ('blk', 'beam'), split_axis=1, concat_axis=1, ti...  17.3 us
  transfers between devices with their start and end apart: 8, of which 5 were waited for; matrix products, arithmetic and copies ran while one was open for 5% of the time, Pallas kernels for 0%

commit v1 on v0

v1 whole, which is shorter than its diff:
```python
import jax
import jax.numpy as jnp
from jax import lax
from jax.experimental import pallas as pl
from jax.experimental.pallas import tpu as pltpu
from jax.sharding import PartitionSpec as P

D = 4096
EPS = 1e-06
MESH = pl.DeviceIdType.MESH
F32, BF16 = jnp.float32, jnp.bfloat16
NZ, NX, NB = 8, 2, 2
NBLK, NALL = NZ * NX, NZ * NX * NB
NY, NC = 4, 2
RB = 16
BLK = 2 * RB
ROWS = NBLK * BLK
HALF = ROWS // 2
INNER = 512
COLS = 256
PREV = 6
CP = 2 * PREV * 2
KP = 8
LANES = 128
SLOTS = 2


def dot(a, b):
    return jnp.dot(a, b, preferred_element_type=F32)


def dot_t(a, b):
    return lax.dot_general(a, b, (((1,), (1,)), ((), ())), preferred_element_type=F32)


def iota(shape, dim):
    return lax.broadcasted_iota(jnp.int32, shape, dim)


def split3(x):
    high = x.astype(BF16).astype(F32)
    middle = (x - high).astype(BF16).astype(F32)
    return high, middle, x - high - middle


def encode(x):
    high, middle, low = split3(x)
    place = iota(x.shape, 1) & 15
    return jnp.where(place < 4, high, jnp.where(place < 8, middle, low)).astype(BF16)


def part_weight(place, lanes):
    return jnp.where(place < 8, 4.0 / lanes, 2.0 / lanes)


def decode_row():
    lane = iota((LANES, LANES), 0)
    return part_weight(lane & 15, LANES).astype(BF16)


def decode_heads():
    lane, col = iota((LANES, INNER), 0), iota((LANES, INNER), 1)
    same = ((lane >> 6) == ((col >> 6) & 1)) & (((lane >> 4) & 3) == (col >> 7))
    return jnp.where(same, part_weight(lane & 15, 16), 0.0).astype(BF16)


def spread_matrix(chosen, pieces, rows, cols):
    rowf = (iota((rows, cols), 0).astype(F32) + 0.5) * (1.0 / pieces)
    piece = (rowf - jnp.floor(rowf)) * pieces
    col_piece = (iota((rows, cols), 1) >> 4).astype(F32)
    keep = jnp.abs(piece - 0.5 - col_piece) < 0.25
    slot_row = iota((rows, NALL * SLOTS), 0)
    slot = iota((rows, NALL * SLOTS), 1) * pieces
    expand = jnp.where((slot_row >= slot) & (slot_row < slot + pieces), 1.0, 0.0).astype(BF16)
    repeat = jnp.where((iota((RB, cols), 1) & 15) == iota((RB, cols), 0), 1.0, 0.0).astype(BF16)
    wide = dot(chosen, repeat).astype(BF16)
    return jnp.where(keep, dot(expand, wide), 0.0).astype(BF16)


def gather_matrix(chosen, pieces, rows, cols):
    colf = (iota((rows, cols), 1).astype(F32) + 0.5) * (1.0 / pieces)
    piece = (colf - jnp.floor(colf)) * pieces
    row_piece = (iota((rows, cols), 0) >> 4).astype(F32)
    keep = jnp.abs(piece - 0.5 - row_piece) < 0.25
    slot_col = iota((NALL * SLOTS, cols), 1)
    slot = iota((NALL * SLOTS, cols), 0) * pieces
    expand = jnp.where((slot_col >= slot) & (slot_col < slot + pieces), 1.0, 0.0).astype(BF16)
    repeat = jnp.where((iota((rows, RB), 0) & 15) == iota((rows, RB), 1), 1.0, 0.0).astype(BF16)
    tall = dot(repeat, chosen).astype(BF16)
    return jnp.where(keep, dot(tall, expand), 0.0).astype(BF16)


def kernel(
    hidden, gains, wqkv, wso, wcq, wco, bias, cache, memory, send_pick, recv_pick,
    out, cache_out,
    hid, xs1, xr1, zs1, zr1, own1, xs2, xr2, zs2, zr2, own2, xs3, xr3, zs3, zr3, own3, lse3,
    hop_send, hop_recv, kv_send, kv_recv, att, query, mixed,
    core_s, core_r, ys, yr, delta, core_s2, core_r2, ys2, yr2, delta2,
    sem_xs, sem_xr, sem_zs, sem_zr, sem_hs, sem_hr, sem_ks, sem_kr, sem_gs, sem_gr, sem_fs, sem_fr,
    sem_cs, sem_cr, sem_ys, sem_yr, sem_ds, sem_dr, sem_es, sem_er,
):
    blk, beam, head = lax.axis_index("blk"), lax.axis_index("beam"), lax.axis_index("head")
    x, z = blk // NZ, lax.rem(blk, NZ)
    y, core = head // NC, lax.rem(head, NC)

    def block_at(dx, dz):
        return (x if dx == 0 else 1 - x) * NZ + lax.rem(z + dz, NZ)

    def z_peer(dz):
        return {"blk": block_at(0, dz)}

    x_peer = {"blk": block_at(1, 0)}

    def all_peer(o):
        where = {"blk": block_at((o // NZ) % NX, o % NZ)}
        if o >= NBLK:
            where["beam"] = 1 - beam
        return where

    core_peer = {"head": y * NC + 1 - core}

    def y_peer(dy):
        return {"head": lax.rem(y + dy, NY) * NC + core}

    def remote(src, dst, send, recv, peer):
        return pltpu.make_async_remote_copy(
            src, dst, send, recv, device_id=peer, device_id_type=MESH
        )

    barrier = pltpu.get_barrier_semaphore()
    peers = [all_peer(o) for o in range(1, NALL)]
    peers += [core_peer] + [y_peer(dy) for dy in range(1, NY)]
    for peer in peers:
        pl.semaphore_signal(barrier, inc=1, device_id=peer, device_id_type=MESH)
    pl.semaphore_wait(barrier, len(peers))

    pending = []

    def x_send(phase, xs, xr):
        for dz in range(NZ):
            copy = remote(xs.at[dz], xr.at[dz], sem_xs.at[phase, dz], sem_xr.at[phase, dz], x_peer)
            copy.start()
            pending.append(copy)

    def x_wait(phase, xs, xr, dz):
        remote(xs.at[dz], xr.at[dz], sem_xs.at[phase, dz], sem_xr.at[phase, dz], x_peer).wait_recv()

    def z_copy(phase, zs, zr, dz):
        return remote(
            zs.at[dz - 1], zr.at[dz - 1], sem_zs.at[phase, dz - 1], sem_zr.at[phase, dz - 1], z_peer(dz)
        )

    far_first = (4, 3, 5, 2, 6, 1, 7)

    def scatter_sums(phase, width, xs, xr, zs, zr, own):
        def joined(dz):
            x_wait(phase, xs, xr, dz)
            rows = pl.ds(dz * BLK, BLK)
            arrived = xr[dz]
            total = own[rows, :width] + arrived[:, :width].astype(F32)
            squares = own[rows, width:] + dot(arrived[:, width:], decode_row())
            return total, squares

        for dz in far_first:
            total, squares = joined(dz)
            zs[dz - 1, :, :width] = total.astype(BF16)
            zs[dz - 1, :, width:] = encode(squares)
            copy = z_copy(phase, zs, zr, dz)
            copy.start()
            pending.append(copy)
        total, squares = joined(0)
        for dz in far_first[::-1]:
            z_copy(phase, zs, zr, dz).wait_recv()
            arrived = zr[dz - 1]
            total += arrived[:, :width].astype(F32)
            squares += dot(arrived[:, width:], decode_row())
        return total, lax.rsqrt(squares[:, :1] / D + EPS)

    def partial_products(states, gain, weight, width, xs, xr, phase, own):
        normed = (states * gain).astype(BF16)
        squares = jnp.sum(states * states, axis=1, keepdims=True)
        squares = jnp.broadcast_to(squares, (ROWS, LANES))
        far = dot(normed[HALF:], weight).astype(BF16)
        code = encode(squares[HALF:])
        for dz in range(NZ):
            xs[dz, :, :width] = far[dz * BLK : (dz + 1) * BLK]
            xs[dz, :, width:] = code[dz * BLK : (dz + 1) * BLK]
        x_send(phase, xs, xr)
        own[:, :width] = dot(normed[:HALF], weight)
        own[:, width:] = squares[:HALF]

    def gather_rows(phase, blocks):
        def copy_z(dz):
            back = (NZ - dz) % NZ
            return remote(
                blocks.at[0], blocks.at[back], sem_gs.at[phase, dz], sem_gr.at[phase, back], z_peer(dz)
            )

        def copy_x(dz):
            return remote(
                blocks.at[dz], blocks.at[NZ + dz], sem_fs.at[phase, dz], sem_fr.at[phase, dz], x_peer
            )

        for dz in far_first:
            copy_z(dz).start()
        copy_x(0).start()
        for dz in far_first[::-1]:
            remote(
                blocks.at[0], blocks.at[dz], sem_gs.at[phase, dz], sem_gr.at[phase, dz], z_peer(dz)
            ).wait_recv()
            copy_x(dz).start()
        for dz in range(NZ):
            copy_x(dz).wait()
        for dz in far_first:
            copy_z(dz).wait_send()
        return blocks[...].reshape(ROWS, INNER)

    def head_sums(phase, product, core_s, core_r, ys, yr, delta):
        mine, other = pl.ds(pl.multiple_of(core * HALF, HALF), HALF), 1 - core
        own2[:, :COLS] = product[:HALF]
        own2[:, COLS:INNER] = product[HALF:]
        first, second = own2[:, :COLS], own2[:, COLS:INNER]
        is_first = core == 0
        core_s[...] = jnp.where(is_first, second, first).astype(BF16)
        copy = remote(core_s, core_r, sem_cs.at[phase], sem_cr.at[phase], core_peer)
        copy.start()
        kept = jnp.where(is_first, first, second)
        copy.wait()
        kept = (kept + core_r[...].astype(F32)).reshape(NY, HALF // NY, COLS)
        own3[:, :COLS] = kept.reshape(HALF, COLS)
        quarter = HALF // NY

        def rows_of(dy):
            return pl.ds(pl.multiple_of(lax.rem(y + dy, NY) * quarter, quarter), quarter)

        order = (2, 1, 3)
        for dy in order:
            ys[dy - 1] = own3[rows_of(dy), :COLS].astype(BF16)
            remote(
                ys.at[dy - 1], yr.at[dy - 1], sem_ys.at[phase, dy - 1], sem_yr.at[phase, dy - 1], y_peer(dy)
            ).start()
        total = own3[rows_of(0), :COLS]
        for dy in (1, 3, 2):
            remote(
                ys.at[dy - 1], yr.at[dy - 1], sem_ys.at[phase, dy - 1], sem_yr.at[phase, dy - 1], y_peer(dy)
            ).wait()
            total += yr[dy - 1].astype(F32)
        delta[0, 0] = total.astype(BF16)

        def copy_y(dy):
            back = (NY - dy) % NY
            return remote(
                delta.at[0, 0], delta.at[0, back], sem_ds.at[phase, dy], sem_dr.at[phase, back], y_peer(dy)
            )

        def copy_c(dy):
            return remote(
                delta.at[0, dy], delta.at[1, dy], sem_es.at[phase, dy], sem_er.at[phase, dy], core_peer
            )

        for dy in order:
            copy_y(dy).start()
        copy_c(0).start()
        for dy in (1, 3, 2):
            remote(
                delta.at[0, 0], delta.at[0, dy], sem_ds.at[phase, dy], sem_dr.at[phase, dy], y_peer(dy)
            ).wait_recv()
            copy_c(dy).start()
        for dy in range(NY):
            copy_c(dy).wait()
        for dy in order:
            copy_y(dy).wait_send()
        for part in range(2):
            half = core if part == 0 else other
            for dy in range(NY):
                start = half * HALF + lax.rem(y + dy, NY) * quarter
                rows = pl.ds(pl.multiple_of(start, quarter), quarter)
                hid[rows, :] += delta[part, dy].astype(F32)

    for o in range(NBLK):
        first = pl.multiple_of(block_at(o // NZ, o % NZ) * RB, RB)
        for t in range(2):
            hid[o * BLK + t * RB : o * BLK + (t + 1) * RB, :] = hidden[t, pl.ds(first, RB), :]
    width1 = 3 * INNER
    partial_products(hid[...], gains[0:1, :], wqkv[...], width1, xs1, xr1, 0, own1)

    def hop_start(step, rows):
        spread = spread_matrix(send_pick[step], CP, NALL * SLOTS * CP, RB * CP)
        hop_send[step] = dot(spread, rows).astype(BF16).reshape(NALL, SLOTS * CP, COLS)
        hop_recv[step, 0] = hop_send[step, 0]
        for o in range(1, NALL):
            copy = remote(
                hop_send.at[step, o], hop_recv.at[step, o], sem_hs.at[step, o], sem_hr.at[step, o], all_peer(o)
            )
            copy.start()
            pending.append(copy)

    def hop_end(step):
        pick = gather_matrix(recv_pick[step], CP, RB * CP, NALL * SLOTS * CP)
        for o in range(1, NALL):
            remote(
                hop_send.at[step, o], hop_recv.at[step, o], sem_hs.at[step, o], sem_hr.at[step, o], all_peer(o)
            ).wait_recv()
        return dot(pick, hop_recv[step].reshape(NALL * SLOTS * CP, COLS)).astype(BF16)

    hop_start(0, cache[...])
    total, scale = scatter_sums(0, width1, xs1, xr1, zs1, zr1, own1)
    qkv = (total * scale).astype(BF16)
    held0 = hop_end(0)
    hop_start(1, held0)

    fresh = qkv[:RB, INNER:]
    stacked = jnp.concatenate([fresh[:, p * LANES : (p + 1) * LANES] for p in range(KP)], axis=0)
    spread = spread_matrix(send_pick[1], KP, NALL * SLOTS * KP, RB * KP)
    kv_send[...] = dot(spread, stacked).astype(BF16).reshape(NALL, SLOTS * KP, LANES)
    kv_recv[0] = kv_send[0]

    def kv_copy(o):
        return remote(kv_send.at[o], kv_recv.at[o], sem_ks.at[o], sem_kr.at[o], all_peer(o))

    for o in range(1, NALL):
        copy = kv_copy(o)
        copy.start()
        pending.append(copy)
    held1 = hop_end(1)
    pick = gather_matrix(recv_pick[1], KP, RB * KP, NALL * SLOTS * KP)
    for o in range(1, NALL):
        kv_copy(o).wait_recv()
    moved = dot(pick, kv_recv[...].reshape(NALL * SLOTS * KP, LANES)).astype(BF16)

    def entry(kv, rows):
        first = kv * KP // 2
        return jnp.concatenate(
            [rows[(first + p) * RB : (first + p + 1) * RB] for p in range(KP // 2)], axis=1
        )

    def position(held, kv, pos):
        first = (kv * PREV + pos) * 2
        return jnp.concatenate([held[(first + c) * RB : (first + c + 1) * RB] for c in range(2)], axis=1)

    own_kv = [
        [qkv[t * RB : (t + 1) * RB, (1 + kv) * INNER : (2 + kv) * INNER] for kv in range(2)]
        for t in range(2)
    ]
    grown = []
    for t, held in enumerate((held0, held1)):
        sides = []
        for kv in range(2):
            side = [position(held, kv, pos) for pos in range(PREV)]
            if t == 1:
                side.append(entry(kv, moved))
            side.append(own_kv[t][kv])
            sides.append(side)
        grown.append(sides)
    for kv in range(2):
        for pos in range(PREV + 2):
            cache_out[kv, pos] = grown[1][kv][pos]

    same_head = (
        (iota((INNER, INNER), 0) >> 6) == (iota((INNER, INNER), 1) >> 6)
    )
    ones = jnp.where(same_head, 1.0, 0.0).astype(BF16)
    for t in range(2):
        keys, values = grown[t]
        q = qkv[t * RB : (t + 1) * RB, :INNER].astype(F32) * 0.125
        products = jnp.concatenate([q * k.astype(F32) for k in keys], axis=0)
        high = products.astype(BF16)
        low = (products - high.astype(F32)).astype(BF16)
        sums = dot(high, ones) + dot(low, ones)
        last = PREV + t
        scores = [
            sums[j * RB : (j + 1) * RB] + bias[last - j : last - j + 1, :] for j in range(last + 1)
        ]
        peak = scores[0]
        for s in scores[1:]:
            peak = jnp.maximum(peak, s)
        weights = [jnp.exp(s - peak) for s in scores]
        whole, acc = weights[0], weights[0].astype(BF16).astype(F32) * values[0].astype(F32)
        for w, v in zip(weights[1:], values[1:]):
            whole += w
            acc += w.astype(BF16).astype(F32) * v.astype(F32)
        att[0, t * RB : (t + 1) * RB, :] = (acc / whole).astype(BF16)
    head_sums(0, dot(gather_rows(0, att), wso[...]), core_s, core_r, ys, yr, delta)

    partial_products(hid[...], gains[1:2, :], wcq[...], INNER, xs2, xr2, 1, own2)
    total, scale = scatter_sums(1, INNER, xs2, xr2, zs2, zr2, own2)
    query[0] = ((total * scale).astype(BF16).astype(F32) * 0.125).astype(BF16)
    queries = gather_rows(1, query)
    tokens = memory.shape[1]
    low_lane = iota((tokens, LANES), 1) < 64
    accs, lses = [], []
    for p in range(INNER // LANES):
        cols = slice(p * LANES, (p + 1) * LANES)
        k, v = memory[0, :, cols].astype(F32), memory[1, :, cols].astype(F32)
        k2 = jnp.concatenate([jnp.where(low_lane, k, 0.0), jnp.where(low_lane, 0.0, k)], axis=0)
        one = jnp.where(low_lane, 1.0, 0.0)
        v2 = jnp.concatenate(
            [
                jnp.concatenate([jnp.where(low_lane, v, 0.0), one], axis=1),
                jnp.concatenate([jnp.where(low_lane, 0.0, v), 1.0 - one], axis=1),
            ],
            axis=0,
        )
        scores = dot_t(queries[:, cols], k2.astype(BF16))
        peak0 = jnp.max(scores[:, :tokens], axis=1, keepdims=True)
        peak1 = jnp.max(scores[:, tokens:], axis=1, keepdims=True)
        weights = jnp.concatenate(
            [jnp.exp(scores[:, :tokens] - peak0), jnp.exp(scores[:, tokens:] - peak1)], axis=1
        )
        both = dot(weights.astype(BF16), v2.astype(BF16))
        low_out = iota((ROWS, LANES), 1) < 64
        lse = jnp.where(low_out, peak0, peak1) + jnp.log(both[:, LANES:])
        acc = both[:, :LANES] / both[:, LANES:]
        own3[:, cols] = acc[:HALF]
        lse3[:, cols] = lse[:HALF]
        far = acc[HALF:].astype(BF16)
        for dz in range(NZ):
            xs3[dz, :, cols] = far[dz * BLK : (dz + 1) * BLK]
        accs.append(None)
        lses.append(lse[HALF:])
    group = (iota((HALF, LANES), 1) >> 4) & 3
    code = jnp.where(group == 0, lses[0], jnp.where(group == 1, lses[1], jnp.where(group == 2, lses[2], lses[3])))
    code = encode(code)
    for dz in range(NZ):
        xs3[dz, :, INNER:] = code[dz * BLK : (dz + 1) * BLK]
    x_send(2, xs3, xr3)

    spread_heads = decode_heads()

    def joined(dz):
        x_wait(2, xs3, xr3, dz)
        rows = pl.ds(dz * BLK, BLK)
        arrived = xr3[dz]
        other = dot(arrived[:, INNER:], spread_heads)
        mine = lse3[rows, :]
        peak = jnp.maximum(mine, other)
        w_mine, w_other = jnp.exp(mine - peak), jnp.exp(other - peak)
        whole = w_mine + w_other
        acc = own3[rows, :INNER] * w_mine + arrived[:, :INNER].astype(F32) * w_other
        return acc / whole, peak + jnp.log(whole)

    for dz in far_first:
        acc, lse = joined(dz)
        zs3[dz - 1, :, :INNER] = acc.astype(BF16)
        place = (iota((BLK, LANES), 1) >> 4) & 3
        four = [lse[:, p * LANES : (p + 1) * LANES] for p in range(4)]
        picked = jnp.where(place == 0, four[0], jnp.where(place == 1, four[1], jnp.where(place == 2, four[2], four[3])))
        zs3[dz - 1, :, INNER:] = encode(picked)
        copy = z_copy(2, zs3, zr3, dz)
        copy.start()
        pending.append(copy)
    acc, peak = joined(0)
    parts = [(acc, peak)]
    for dz in far_first[::-1]:
        z_copy(2, zs3, zr3, dz).wait_recv()
        arrived = zr3[dz - 1]
        parts.append((arrived[:, :INNER].astype(F32), dot(arrived[:, INNER:], spread_heads)))
        peak = jnp.maximum(peak, parts[-1][1])
    weights = [jnp.exp(l - peak) for _, l in parts]
    acc, whole = parts[0][0] * weights[0], weights[0]
    for (a, _), w in zip(parts[1:], weights[1:]):
        acc += a * w
        whole += w
    mixed[0] = (acc / whole).astype(BF16)
    head_sums(1, dot(gather_rows(2, mixed), wco[...]), core_s2, core_r2, ys2, yr2, delta2)

    for o in range(NBLK):
        first = pl.multiple_of(block_at(o // NZ, o % NZ) * RB, RB)
        for t in range(2):
            out[t, pl.ds(first, RB), :] = hid[o * BLK + t * RB : o * BLK + (t + 1) * RB, :]
    for copy in pending:
        copy.wait_send()


def picks(parent_list):
    blk, beam = lax.axis_index("blk"), lax.axis_index("beam")
    x, z = blk // NZ, blk % NZ
    me = beam * NBLK + blk
    o = jnp.arange(NALL, dtype=jnp.int32)
    at_offset = (beam ^ o // NBLK) * NBLK + (x ^ (o // NZ) % NX) * NZ + (z + o % NZ) % NZ
    placed = at_offset[:, None] == jnp.arange(NALL, dtype=jnp.int32)
    blocks = jnp.sum(jnp.where(placed[:, :, None], parent_list.reshape(1, NALL, RB), 0), axis=1)
    source, local = blocks // RB, blocks % RB
    order = jnp.arange(RB, dtype=jnp.int32)
    same = source[:, :, None] == source[:, None, :]
    slot = jnp.sum((same & (order[None, :] < order[:, None])[None]).astype(jnp.int32), axis=2)
    entries = (source == me)[:, None, :] & (slot[:, None, :] == jnp.arange(SLOTS, dtype=jnp.int32)[None, :, None])
    chosen = entries[:, :, :, None] & (local[:, None, :, None] == order)
    send = jnp.any(chosen, axis=2).reshape(NALL * SLOTS, RB)
    own_source = source[0]
    sb, sx, sz = own_source // NBLK, (own_source // NZ) % NX, own_source % NZ
    offset = (sb ^ beam) * NBLK + (sx ^ x) * NZ + (z - sz + NZ) % NZ
    recv = (offset * SLOTS + slot[0])[:, None] == jnp.arange(NALL * SLOTS, dtype=jnp.int32)
    return send.astype(BF16), recv.astype(BF16)


def body(
    hidden_in, norm_gains, w_qkv, w_self_out, w_cross_q, w_cross_out, pos_bias, self_cache, memory, parents
):
    steps = [picks(parents[t]) for t in range(2)]
    send_pick = jnp.stack([s for s, _ in steps])
    recv_pick = jnp.stack([r for _, r in steps])
    bias = jnp.repeat(pos_bias.T, 64, axis=1)
    cache = self_cache[:, 0].reshape(2, RB, PREV, 2, COLS).transpose(0, 2, 3, 1, 4).reshape(CP * RB, COLS)
    dma = pltpu.SemaphoreType.DMA

    def exchange(width):
        wide = width + LANES
        return [
            pltpu.VMEM((NZ, BLK, wide), BF16),
            pltpu.VMEM((NZ, BLK, wide), BF16),
            pltpu.VMEM((NZ - 1, BLK, wide), BF16),
            pltpu.VMEM((NZ - 1, BLK, wide), BF16),
            pltpu.VMEM((HALF, wide), F32),
        ]

    head_buffers = [
        pltpu.VMEM((HALF, COLS), BF16),
        pltpu.VMEM((HALF, COLS), BF16),
        pltpu.VMEM((NY - 1, HALF // NY, COLS), BF16),
        pltpu.VMEM((NY - 1, HALF // NY, COLS), BF16),
        pltpu.VMEM((2, NY, HALF // NY, COLS), BF16),
    ]
    in_vmem = pl.BlockSpec(memory_space=pltpu.VMEM)
    hidden_out, cache_rows = pl.pallas_call(
        kernel,
        out_shape=(
            jax.ShapeDtypeStruct(hidden_in.shape, F32),
            jax.ShapeDtypeStruct((2, PREV + 2, RB, INNER), BF16),
        ),
        in_specs=[in_vmem] * 11,
        out_specs=(in_vmem, in_vmem),
        scratch_shapes=[
            pltpu.VMEM((ROWS, COLS), F32),
            *exchange(3 * INNER),
            *exchange(INNER),
            *exchange(INNER),
            pltpu.VMEM((HALF, INNER), F32),
            pltpu.VMEM((2, NALL, SLOTS * CP, COLS), BF16),
            pltpu.VMEM((2, NALL, SLOTS * CP, COLS), BF16),
            pltpu.VMEM((NALL, SLOTS * KP, LANES), BF16),
            pltpu.VMEM((NALL, SLOTS * KP, LANES), BF16),
            *[pltpu.VMEM((NBLK, BLK, INNER), BF16)] * 3,
            *head_buffers,
            *head_buffers,
            dma((3, NZ)), dma((3, NZ)), dma((3, NZ - 1)), dma((3, NZ - 1)),
            dma((2, NALL)), dma((2, NALL)), dma((NALL,)), dma((NALL,)),
            dma((3, NZ)), dma((3, NZ)), dma((3, NZ)), dma((3, NZ)),
            dma((2,)), dma((2,)), dma((2, NY - 1)), dma((2, NY - 1)),
            dma((2, NY)), dma((2, NY)), dma((2, NY)), dma((2, NY)),
        ],
        compiler_params=pltpu.CompilerParams(
            collective_id=0, has_side_effects=True, vmem_limit_bytes=58 * 1024 * 1024
        ),
        name="decode",
    )(
        hidden_in, norm_gains, w_qkv.reshape(COLS, 3 * INNER), w_self_out, w_cross_q, w_cross_out,
        bias, cache, memory, send_pick, recv_pick,
    )
    return hidden_out, cache_rows.transpose(0, 2, 1, 3)[:, None]


def solution(mesh):
    placed = (
        P(None, "beam", "blk"),
        P(None, "blk"),
        P("blk", None, "head"),
        P("head", "blk"),
        P("blk", "head"),
        P("head", "blk"),
        P("head", None),
        P(None, "beam", "blk", None, "head"),
        P(None, "blk", "head"),
        P(),
    )
    return jax.shard_map(
        body,
        mesh=mesh,
        in_specs=placed,
        out_specs=(P(None, "beam", "blk"), P(None, "beam", "blk", None, "head")),
        check_vma=False,
    )
```

time: 721 us -> 189 us (0.26)
  waiting for transfers between devices: 362 us -> 0 us
  blocking collectives: 236 us -> 0 us
  Pallas kernels: 0 us -> 177 us
  local copies, waits for them, and re-layouts: 49.8 us -> 8.02 us
  other arithmetic: 24.3 us -> 3.01 us
  starting transfers between devices: 17.8 us -> 0 us
  between operations: 14.9 us -> 0.8 us
  matrix products: 13.2 us -> 0 us
    psum x4 -> x0, waiting for transfers between devices: 335 us -> none  [the longest x2 185 us: project(): summed, square_sum = lax.psum((partial_sum, squares), 'blk')]
    pallas_call x0 -> x1, Pallas kernels: none -> 177 us  [body(): pl.pallas_call(kernel, out_shape=(jax.ShapeDtypeStruct(hidden_in.shape, F...]
    all_gather x6 -> x0, blocking collectives: 159 us -> none  [the longest x4 101 us: combined_all(): lax.all_gather(a.astype(kind), axis)]
    psum x2 -> x0, blocking collectives: 76.6 us -> none  [project(): summed, square_sum = lax.psum((partial_sum, squares), 'blk')]
    dynamic_slice x62 -> x0, local copies, waits for them, and re-layouts: 33.4 us -> none  [the longest x60 33.3 us: take(): lax.dynamic_index_in_dim(a, source, 0, False).astype(own.dtype)]
    all_gather x2 -> x0, waiting for transfers between devices: 27 us -> none  [combined_all(): lax.all_gather(a.astype(kind), axis)]
    all_to_all x2 -> x0, starting transfers between devices: 17.3 us -> none  [reorder(): lax.all_to_all(outgoing, ('blk', 'beam'), split_axis=1, concat_axis=1, ti...]
    dot_general x16 -> x0, matrix products: 13.2 us -> none  [the longest x4 7.11 us: project(): partial_sum = jnp.dot(normed, weight, preferred_element_type=jnp.float32)]
  transfers between devices with their start and end apart: 8 -> 0, of which waited for: 5 -> 0; matrix products, arithmetic and copies ran while one was open for 5% -> 0% of each run, Pallas kernels for 0% -> 0%
where the time goes in v1:
time: 189 us
  Pallas kernels  177 us (94%)
  local copies, waits for them, and re-layouts  8.02 us (4%)
  other arithmetic  3.01 us (2%)
    pallas_call x1, Pallas kernels, body(): pl.pallas_call(kernel, out_shape=(jax.ShapeDtypeStruct(hidden_in.shape, F...  177 us
    unnamed x13, local copies, waits for them, and re-layouts  4.13 us

profile of v1, /device:TPU:1, one launch (start us, length us, event | category | flops | bytes accessed | tf_op | source)
XLA Modules:
  0.0 188.8 jit_solution(5256624593000511710)
XLA Ops:
  0.7 0.0 copy-start.3
  0.7 0.1 iota_compare_fusion.4
  0.8 0.6 copy-done.3
  1.3 0.0 copy-start.4
  1.3 0.1 copy.81
  1.4 0.6 copy-done.4
  2.1 0.0 copy-start.2
  2.1 0.1 broadcast_in_dim.39
  2.1 0.0 copy-start
  2.1 0.1 copy.83
  2.2 0.1 broadcast_in_dim.42
  2.3 0.1 copy.89
  2.4 1.2 select_reduce_fusion.1
  3.5 0.1 copy.84
  3.6 0.1 copy.90
  3.7 0.1 slice_reduce_fusion.1
  3.9 0.1 slice_reduce_fusion.3
  4.0 0.1 convert_reduce_fusion.1
  4.1 0.1 slice_reduce_fusion.2
  4.2 0.1 slice_reduce_fusion
  4.4 0.1 iota_compare_fusion.5
  4.5 0.1 iota_compare_fusion.6
  4.5 0.6 add_convert_fusion.1.recv_pick
  5.2 0.1 copy.88
  5.4 0.1 copy.94
  5.6 0.6 add_convert_fusion.send_pick
  6.2 0.1 broadcast_in_dim.37
  6.3 0.7 reshape.507.bias
  7.0 0.0 copy-done.2
  7.0 0.1 reshape_squeeze.2
  7.0 0.7 copy.82
  7.7 0.0 copy-done
  7.7 0.3 copy.80
  8.0 1.2 copy.95.wqkv
  9.2 177.0 %decode.1 = (f32[2,256,256]{2,1,0:T(8,128)}, bf16[2,8,16,512]{3,2,1,0:T(8,128)(2,1)}) custom-call(f32[2,256,256]{2,1,0:T(8,128)} %hidden.1, f32[2,256]{1,0:T(2,128)} %gains.1, bf16[256,1536]{1,0:T(8,128)(2,1)} %copy.95.wqkv, bf16[512,256]{1,0:T(8,128)(2,1)} %wso.1, bf16[256,512]{1,0:T(8,128)(2,1)} %wcq.1, bf16[512,256]{1,0:T(8,128)(2,1)} %wco.1, ...), custom_call_target="tpu_custom_call" | custom-call | tf_op jit(solution)/shard_map/decode/pallas_call | solution.py:525
  186.1 0.0 copy-start.1
  186.1 1.9 copy.96
  188.0 0.0 copy-done.1
  188.0 0.8 copy.98
  (15 shorter events, 0.3 us)
Async XLA Ops:
  0.7 0.7 copy-start.3
  1.3 0.7 copy-start.4
  2.1 4.9 %copy-start.2 = (bf16[2,1,16,6,512]{4,2,3,1,0:T(8,128)(2,1)S(1)}, bf16[2,1,16,6,512]{4,2,3,1,0:T(8,128)(2,1)}, u32[]{:S(2)}) copy-start(bf16[2,1,16,6,512]{4,2,3,1,0:T(8,128)(2,1)} %param.17) | copy-start | bytes 589828
  2.1 5.6 %copy-start = (bf16[256,3,512]{2,0,1:T(8,128)(2,1)S(1)}, bf16[256,3,512]{2,0,1:T(8,128)(2,1)}, u32[]{:S(2)}) copy-start(bf16[256,3,512]{2,0,1:T(8,128)(2,1)} %param.12) | copy-start | bytes 2359300
  186.1 1.9 copy-start.1

commit v2 on v0

v2 whole, which is shorter than its diff:
```python
import jax
import jax.numpy as jnp
from jax import lax
from jax.experimental import pallas as pl
from jax.experimental.pallas import tpu as pltpu
from jax.sharding import PartitionSpec as P

D = 4096
EPS = 1e-06
MESH = pl.DeviceIdType.MESH
F32, BF16 = jnp.float32, jnp.bfloat16
NZ, NX, NB = 8, 2, 2
NBLK, NALL = NZ * NX, NZ * NX * NB
NY, NC = 4, 2
RB = 16
BLK = 2 * RB
ROWS = NZ * BLK
HALF = ROWS // 2
INNER = 512
COLS = 256
WIDE = 2 * COLS
SPLIT = 144
PREV = 6
CP = 2 * PREV * 2
KP = 8
LANES = 128
SLOTS = 2


def dot(a, b):
    return jnp.dot(a, b, preferred_element_type=F32)


def dot_t(a, b):
    return lax.dot_general(a, b, (((1,), (1,)), ((), ())), preferred_element_type=F32)


def iota(shape, dim):
    return lax.broadcasted_iota(jnp.int32, shape, dim)


def split3(x):
    high = x.astype(BF16).astype(F32)
    middle = (x - high).astype(BF16).astype(F32)
    return high, middle, x - high - middle


def encode(x):
    high, middle, low = split3(x)
    place = iota(x.shape, 1) & 15
    return jnp.where(place < 4, high, jnp.where(place < 8, middle, low)).astype(BF16)


def part_weight(place, lanes):
    return jnp.where(place < 8, 4.0 / lanes, 2.0 / lanes)


def decode_row():
    lane = iota((LANES, LANES), 0)
    return part_weight(lane & 15, LANES).astype(BF16)


def decode_heads():
    lane, col = iota((LANES, INNER), 0), iota((LANES, INNER), 1)
    same = ((lane >> 6) == ((col >> 6) & 1)) & (((lane >> 4) & 3) == (col >> 7))
    return jnp.where(same, part_weight(lane & 15, 16), 0.0).astype(BF16)


def piece_mask(shape, dim, pieces):
    place = (iota(shape, dim).astype(F32) + 0.5) * (1.0 / pieces)
    piece = (place - jnp.floor(place)) * pieces - 0.5
    return jnp.abs(piece - (iota(shape, 1 - dim) >> 4).astype(F32)) < 0.25


def slot_matrix(shape, dim, pieces):
    q = iota(shape, 1 - dim)
    first = ((q & (NALL - 1)) * SLOTS + (q >> 5)) * pieces
    place = iota(shape, dim)
    return jnp.where((place >= first) & (place < first + pieces), 1.0, 0.0).astype(BF16)


def spread_matrix(chosen, pieces):
    rows, cols = NALL * SLOTS * pieces, RB * pieces
    repeat = jnp.where((iota((RB, cols), 1) & 15) == iota((RB, cols), 0), 1.0, 0.0).astype(BF16)
    full = dot(slot_matrix((rows, NALL * SLOTS), 0, pieces), dot(chosen, repeat).astype(BF16))
    return jnp.where(piece_mask((rows, cols), 0, pieces), full, 0.0).astype(BF16)


def gather_matrix(chosen, pieces):
    rows, cols = RB * pieces, NALL * SLOTS * pieces
    repeat = jnp.where((iota((rows, RB), 0) & 15) == iota((rows, RB), 1), 1.0, 0.0).astype(BF16)
    full = dot(dot_t(repeat, chosen).astype(BF16), slot_matrix((NALL * SLOTS, cols), 1, pieces))
    return jnp.where(piece_mask((rows, cols), 1, pieces), full, 0.0).astype(BF16)


def picks(parents, x, z, beam):
    square = (NALL, NALL)
    o, block = iota(square, 0), iota(square, 1)
    flip_x, flip_b = (o >> 3) & 1, o >> 4
    at_offset = (beam + flip_b - 2 * beam * flip_b) * NBLK + (x + flip_x - 2 * x * flip_x) * NZ + ((z + o) & 7)
    permute = jnp.where(at_offset == block, 1.0, 0.0).astype(BF16)
    source = dot(permute, (parents >> 4).astype(F32).astype(BF16))
    local = dot(permute, (parents & 15).astype(F32).astype(BF16))
    lane = iota((NALL, RB), 1)
    slot = jnp.zeros((NALL, RB), F32)
    for k in range(RB - 1):
        slot += jnp.where((source[:, k : k + 1] == source) & (lane > k), 1.0, 0.0)
    me = (beam * NBLK + x * NZ + z).astype(F32)
    send = []
    for s in range(SLOTS):
        mine = jnp.where((source == me) & (slot == s), local, -1.0)
        send.append(sum(jnp.where(mine[:, k : k + 1] == lane.astype(F32), 1.0, 0.0) for k in range(RB)))
    own = source[:1].astype(jnp.int32)
    own_b, own_x, own_z = own >> 4, (own >> 3) & 1, own & 7
    differ_b, differ_x = jnp.abs(own_b - beam), jnp.abs(own_x - x)
    offset = differ_b * NBLK + differ_x * NZ + ((z - own_z + NZ) & 7) + slot[:1].astype(jnp.int32) * NALL
    q = iota((NALL * SLOTS, RB), 0)
    recv = jnp.where(q == offset, 1.0, 0.0)
    return jnp.concatenate(send, axis=0).astype(BF16), recv.astype(BF16)


def kernel(
    hidden, gains, wqkv, wso, wcq, wco, bias, cache, memory, parents,
    out, cache_out,
    far_hid, near_hid, far_gain, near_gain, far_wqkv, far_wso, far_wcq, far_wco, far_memory,
    hid, summed, prod, zs1, zr1, own1, zs2, zr2, own2, zs3, zr3,
    hop_send, hop_recv, kv_send, kv_recv, att, query, mixed, last_s, last_r,
    core_s, core_r, ys, yr, delta, core_s2, core_r2, ys2, yr2, delta2,
    sem_ws, sem_wr, sem_zs, sem_zr, sem_hs, sem_hr, sem_ks, sem_kr, sem_gs, sem_gr,
    sem_cs, sem_cr, sem_ys, sem_yr, sem_ds, sem_dr, sem_es, sem_er,
):
    blk, beam, head = lax.axis_index("blk"), lax.axis_index("beam"), lax.axis_index("head")
    x, z = blk // NZ, lax.rem(blk, NZ)
    y, core = head // NC, lax.rem(head, NC)

    def block_at(dx, dz):
        return (x if dx == 0 else 1 - x) * NZ + lax.rem(z + dz, NZ)

    def z_peer(dz):
        return {"blk": block_at(0, dz)}

    def all_peer(o):
        where = {"blk": block_at((o // NZ) % NX, o % NZ)}
        if o >= NBLK:
            where["beam"] = 1 - beam
        return where

    pair_peer = all_peer(NZ)
    other_peer = all_peer(NBLK + NZ)
    core_peer = {"head": y * NC + 1 - core}

    def y_peer(dy):
        return {"head": lax.rem(y + dy, NY) * NC + core}

    def remote(src, dst, send, recv, peer):
        return pltpu.make_async_remote_copy(
            src, dst, send, recv, device_id=peer, device_id_type=MESH
        )

    def rows_at(dx, dz):
        return pl.ds(pl.multiple_of(block_at(dx, dz) * RB, RB), RB)

    with jax.named_scope("entry_barrier"):
        barrier = pltpu.get_barrier_semaphore()
        peers = [all_peer(o) for o in range(1, NALL)]
        peers += [core_peer] + [y_peer(dy) for dy in range(1, NY)]
        for peer in peers:
            pl.semaphore_signal(barrier, inc=1, device_id=peer, device_id_type=MESH)
        for dz in range(NZ):
            for t in range(2):
                rows = slice(dz * BLK + t * RB, dz * BLK + (t + 1) * RB)
                far_hid[rows, :] = hidden[t, rows_at(1, dz), :]
                hid[rows, :COLS] = hidden[t, rows_at(0, dz), :]
        far_gain[...] = jnp.zeros_like(far_gain)
        far_gain[:2, :] = gains[...]
        pl.semaphore_wait(barrier, len(peers))

    pending = []

    def begin(copy):
        copy.start()
        pending.append(copy)

    my_half = pl.ds(pl.multiple_of(core * HALF, HALF), HALF)
    its_half = pl.ds(pl.multiple_of((1 - core) * HALF, HALF), HALF)

    def pair_copy(i, src, dst, peer):
        return remote(src, dst, sem_ws.at[i], sem_wr.at[i], peer)

    early = [
        pair_copy(0, far_hid.at[my_half], near_hid.at[my_half], pair_peer),
        pair_copy(1, far_gain, near_gain, pair_peer),
        pair_copy(2, wqkv.at[:, pl.ds(0, SPLIT)], far_wqkv.at[:, pl.ds(0, SPLIT)], other_peer),
        pair_copy(3, wqkv.at[:, pl.ds(SPLIT, COLS - SPLIT)], far_wqkv.at[:, pl.ds(SPLIT, COLS - SPLIT)], pair_peer),
    ]
    late = [
        pair_copy(4, wso, far_wso, other_peer),
        pair_copy(5, wcq, far_wcq, pair_peer),
        pair_copy(6, memory, far_memory, other_peer),
        pair_copy(7, wco, far_wco, pair_peer),
    ]
    for copy in early:
        begin(copy)

    def hop_copy(step, o):
        return remote(
            hop_send.at[step, o], hop_recv.at[step, o], sem_hs.at[step, o], sem_hr.at[step, o], all_peer(o)
        )

    def hop_start(step, chosen, rows):
        picked = dot(spread_matrix(chosen, CP), rows).astype(BF16)
        hop_send[step] = picked.reshape(NALL, SLOTS * CP, COLS)
        hop_recv[step, 0] = hop_send[step, 0]
        for o in range(1, NALL):
            begin(hop_copy(step, o))

    def hop_end(step, chosen):
        pick = gather_matrix(chosen, CP)
        for o in range(1, NALL):
            hop_copy(step, o).wait_recv()
        return dot(pick, hop_recv[step].reshape(NALL * SLOTS * CP, COLS)).astype(BF16)

    with jax.named_scope("cache_send"):
        send0, recv0 = picks(parents[0], x, z, beam)
        pieces = [
            cache[kv, pos, :, c * COLS : (c + 1) * COLS] for kv in range(2) for pos in range(PREV) for c in range(2)
        ]
        hop_start(0, send0, jnp.concatenate(pieces, axis=0))
        for copy in late:
            begin(copy)
        send1, recv1 = picks(parents[1], x, z, beam)

    def z_copy(phase, zs, zr, dz):
        return remote(
            zs.at[dz - 1], zr.at[dz - 1], sem_zs.at[phase, dz - 1], sem_zr.at[phase, dz - 1], z_peer(dz)
        )

    far_first = (4, 3, 5, 2, 6, 1, 7)

    def scatter_sums(phase, width, zs, zr, own):
        for dz in far_first:
            rows = slice(dz * BLK, (dz + 1) * BLK)
            zs[dz - 1, :, :width] = own[rows, :width].astype(BF16)
            zs[dz - 1, :, width:] = encode(own[rows, width:])
            begin(z_copy(phase, zs, zr, dz))
        total, squares = own[:BLK, :width], own[:BLK, width:]
        for dz in far_first[::-1]:
            z_copy(phase, zs, zr, dz).wait_recv()
            arrived = zr[dz - 1]
            total += arrived[:, :width].astype(F32)
            squares += dot(arrived[:, width:], decode_row())
        return total, lax.rsqrt(squares[:, :1] / D + EPS)

    def square_sums(states):
        return jnp.broadcast_to(jnp.sum(states * states, axis=1, keepdims=True), (ROWS, LANES))

    def gather_rows(phase, blocks):
        def copy(dz):
            back = NZ - dz
            return remote(
                blocks.at[0], blocks.at[back], sem_gs.at[phase, dz], sem_gr.at[phase, back], z_peer(dz)
            )

        for dz in far_first:
            begin(copy(dz))
        for dz in far_first[::-1]:
            remote(
                blocks.at[0], blocks.at[dz], sem_gs.at[phase, dz], sem_gr.at[phase, dz], z_peer(dz)
            ).wait_recv()
        return blocks[...].reshape(ROWS, INNER)

    quarter = HALF // NY

    def quarter_rows(half, dy):
        start = half * HALF + lax.rem(y + dy, NY) * quarter
        return pl.ds(pl.multiple_of(start, quarter), quarter)

    def head_sums(phase, core_s, core_r, ys, yr, delta):
        core_s[...] = prod[its_half, :].astype(BF16)
        copy = remote(core_s, core_r, sem_cs.at[phase], sem_cr.at[phase], core_peer)
        begin(copy)
        copy.wait_recv()
        prod[my_half, :] += core_r[...].astype(F32)

        def copy_sum(dy):
            return remote(
                ys.at[dy - 1], yr.at[dy - 1], sem_ys.at[phase, dy - 1], sem_yr.at[phase, dy - 1], y_peer(dy)
            )

        order = (2, 1, 3)
        for dy in order:
            ys[dy - 1] = prod[quarter_rows(core, dy), :].astype(BF16)
            begin(copy_sum(dy))
        total = prod[quarter_rows(core, 0), :]
        for dy in (1, 3, 2):
            copy_sum(dy).wait_recv()
            total += yr[dy - 1].astype(F32)
        delta[0, 0] = total.astype(BF16)

        def copy_y(dy):
            back = NY - dy
            return remote(
                delta.at[0, 0], delta.at[0, back], sem_ds.at[phase, dy], sem_dr.at[phase, back], y_peer(dy)
            )

        def copy_c(dy):
            return remote(
                delta.at[0, dy], delta.at[1, dy], sem_es.at[phase, dy], sem_er.at[phase, dy], core_peer
            )

        for dy in order:
            begin(copy_y(dy))
        begin(copy_c(0))
        for dy in (1, 3, 2):
            remote(
                delta.at[0, 0], delta.at[0, dy], sem_ds.at[phase, dy], sem_dr.at[phase, dy], y_peer(dy)
            ).wait_recv()
            begin(copy_c(dy))
        for dy in range(NY):
            copy_c(dy).wait_recv()
        for part in range(2):
            half = core if part == 0 else 1 - core
            for dy in range(NY):
                added = delta[part, dy].astype(F32)
                hid[quarter_rows(half, dy), :] += added
                if phase == 0:
                    summed[quarter_rows(half, dy), :] = added[:, COLS:]
                else:
                    summed[quarter_rows(half, dy), :] += added[:, COLS:]

    with jax.named_scope("qkv_products"):
        width1 = 3 * INNER
        states = hid[:, :COLS]
        normed = (states * gains[0:1, :]).astype(BF16)
        for j in range(3):
            own1[:, j * INNER : (j + 1) * INNER] = dot(normed, wqkv[j])
        own1[:, width1:] = square_sums(states)
        early[0].wait_recv()
        swap = remote(near_hid.at[my_half], near_hid.at[my_half], sem_ws.at[8], sem_wr.at[8], core_peer)
        begin(swap)
        remote(near_hid.at[my_half], near_hid.at[its_half], sem_ws.at[8], sem_wr.at[8], core_peer).wait_recv()
        early[1].wait_recv()
        states = near_hid[...]
        hid[:, COLS:] = states
        normed = (states * near_gain[0:1, :]).astype(BF16)
        own1[:, width1:] += square_sums(states)
        early[2].wait_recv()
        early[3].wait_recv()
        for j in range(3):
            own1[:, j * INNER : (j + 1) * INNER] += dot(normed, far_wqkv[j])

    with jax.named_scope("qkv_sums"):
        total, scale = scatter_sums(0, width1, zs1, zr1, own1)
        qkv = (total * scale).astype(BF16)

    with jax.named_scope("cache_forward"):
        held0 = hop_end(0, recv0)
        hop_start(1, send1, held0)

    def kv_copy(o):
        return remote(kv_send.at[o], kv_recv.at[o], sem_ks.at[o], sem_kr.at[o], all_peer(o))

    with jax.named_scope("entry_send"):
        fresh = qkv[:RB, INNER:]
        stacked = jnp.concatenate([fresh[:, p * LANES : (p + 1) * LANES] for p in range(KP)], axis=0)
        kv_send[...] = dot(spread_matrix(send1, KP), stacked).astype(BF16).reshape(NALL, SLOTS * KP, LANES)
        kv_recv[0] = kv_send[0]
        for o in range(1, NALL):
            begin(kv_copy(o))

    with jax.named_scope("cache_last"):
        held1 = hop_end(1, recv1)

    with jax.named_scope("entry_receive"):
        pick = gather_matrix(recv1, KP)
        for o in range(1, NALL):
            kv_copy(o).wait_recv()
        moved = dot(pick, kv_recv[...].reshape(NALL * SLOTS * KP, LANES)).astype(BF16)

    def side_by_side(rows, first, count):
        return jnp.concatenate([rows[(first + p) * RB : (first + p + 1) * RB] for p in range(count)], axis=1)

    with jax.named_scope("self_attention"):
        grown = []
        for t, held in enumerate((held0, held1)):
            sides = []
            for kv in range(2):
                side = [side_by_side(held, (kv * PREV + pos) * 2, 2) for pos in range(PREV)]
                if t == 1:
                    side.append(side_by_side(moved, kv * KP // 2, KP // 2))
                side.append(qkv[t * RB : (t + 1) * RB, (1 + kv) * INNER : (2 + kv) * INNER])
                sides.append(side)
            grown.append(sides)
        same_head = (iota((INNER, INNER), 0) >> 6) == (iota((INNER, INNER), 1) >> 6)
        ones = jnp.where(same_head, 1.0, 0.0).astype(BF16)
        of_head = jnp.where((iota((8, INNER), 1) >> 6) == iota((8, INNER), 0), 1.0, 0.0).astype(BF16)
        wide_bias = sum(dot(part.astype(BF16), of_head) for part in split3(bias[...]))
        for t in range(2):
            keys, values = grown[t]
            q = qkv[t * RB : (t + 1) * RB, :INNER].astype(F32) * 0.125
            products = jnp.concatenate([q * k.astype(F32) for k in keys], axis=0)
            high = products.astype(BF16)
            low = (products - high.astype(F32)).astype(BF16)
            sums = dot(high, ones) + dot(low, ones)
            last = PREV + t
            scores = [
                sums[j * RB : (j + 1) * RB] + wide_bias[last - j : last - j + 1, :] for j in range(last + 1)
            ]
            peak = scores[0]
            for s in scores[1:]:
                peak = jnp.maximum(peak, s)
            weights = [jnp.exp(s - peak) for s in scores]
            whole, acc = weights[0], weights[0].astype(BF16).astype(F32) * values[0].astype(F32)
            for w, v in zip(weights[1:], values[1:]):
                whole += w
                acc += w.astype(BF16).astype(F32) * v.astype(F32)
            att[0, t * RB : (t + 1) * RB, :] = (acc / whole).astype(BF16)

    with jax.named_scope("self_out"):
        rows = gather_rows(0, att)
        late[0].wait_recv()
        prod[:, :COLS] = dot(rows, wso[...])
        prod[:, COLS:] = dot(rows, far_wso[...])
        head_sums(0, core_s, core_r, ys, yr, delta)

    with jax.named_scope("cross_query_products"):
        states = hid[...]
        gain = jnp.concatenate([gains[1:2, :], near_gain[1:2, :]], axis=1)
        normed = (states * gain).astype(BF16)
        late[1].wait_recv()
        own2[:, :INNER] = dot(normed[:, :COLS], wcq[...]) + dot(normed[:, COLS:], far_wcq[...])
        own2[:, INNER:] = square_sums(states)

    with jax.named_scope("cross_query_sums"):
        total, scale = scatter_sums(1, INNER, zs2, zr2, own2)
        query[0] = ((total * scale).astype(BF16).astype(F32) * 0.125).astype(BF16)

    with jax.named_scope("cross_query_gather"):
        place = iota((RB * (PREV + 2), RB * (PREV + 2)), 0)
        from_row = (place & 7) * RB + (place >> 3)
        turn = jnp.where(from_row == iota(place.shape, 1), 1.0, 0.0).astype(BF16)
        queries = gather_rows(1, query)
        for kv in range(2):
            cache_out[kv] = dot(turn, jnp.concatenate(grown[1][kv], axis=0)).astype(BF16)

    with jax.named_scope("cross_partial"):
        late[2].wait_recv()
        tokens = 2 * memory.shape[1]
        low_lane = iota((tokens, LANES), 1) < 64
        low_out = iota((ROWS, LANES), 1) < 64
        one = jnp.where(low_lane, 1.0, 0.0)
        accs, lses = [], []
        for p in range(INNER // LANES):
            cols = slice(p * LANES, (p + 1) * LANES)
            k, v = (
                jnp.concatenate([memory[kv, :, cols], far_memory[kv, :, cols]], axis=0).astype(F32)
                for kv in range(2)
            )
            k2 = jnp.concatenate([jnp.where(low_lane, k, 0.0), jnp.where(low_lane, 0.0, k)], axis=0)
            v2 = jnp.concatenate(
                [
                    jnp.concatenate([jnp.where(low_lane, v, 0.0), one], axis=1),
                    jnp.concatenate([jnp.where(low_lane, 0.0, v), 1.0 - one], axis=1),
                ],
                axis=0,
            )
            scores = dot_t(queries[:, cols], k2.astype(BF16))
            peak0 = jnp.max(scores[:, :tokens], axis=1, keepdims=True)
            peak1 = jnp.max(scores[:, tokens:], axis=1, keepdims=True)
            weights = jnp.concatenate(
                [jnp.exp(scores[:, :tokens] - peak0), jnp.exp(scores[:, tokens:] - peak1)], axis=1
            )
            both = dot(weights.astype(BF16), v2.astype(BF16))
            lses.append(jnp.where(low_out, peak0, peak1) + jnp.log(both[:, LANES:]))
            acc = both[:, :LANES] / both[:, LANES:]
            accs.append(acc[:BLK])
            narrow = acc.astype(BF16)
            for dz in range(1, NZ):
                zs3[dz - 1, :, cols] = narrow[dz * BLK : (dz + 1) * BLK]
        group = (iota((ROWS, LANES), 1) >> 4) & 3
        low_pair, high_pair = jnp.where(group == 0, lses[0], lses[1]), jnp.where(group == 2, lses[2], lses[3])
        code = encode(jnp.where(group < 2, low_pair, high_pair))
        for dz in range(1, NZ):
            zs3[dz - 1, :, INNER:] = code[dz * BLK : (dz + 1) * BLK]

    with jax.named_scope("cross_join"):
        for dz in far_first:
            begin(z_copy(2, zs3, zr3, dz))
        spread_heads = decode_heads()
        peak = jnp.concatenate([lse[:BLK] for lse in lses], axis=1)
        parts = [(jnp.concatenate(accs, axis=1), peak)]
        for dz in far_first[::-1]:
            z_copy(2, zs3, zr3, dz).wait_recv()
            arrived = zr3[dz - 1]
            parts.append((arrived[:, :INNER].astype(F32), dot(arrived[:, INNER:], spread_heads)))
            peak = jnp.maximum(peak, parts[-1][1])
        weights = [jnp.exp(lse - peak) for _, lse in parts]
        acc, whole = parts[0][0] * weights[0], weights[0]
        for (a, _), w in zip(parts[1:], weights[1:]):
            acc += a * w
            whole += w
        mixed[0] = (acc / whole).astype(BF16)

    with jax.named_scope("cross_out"):
        rows = gather_rows(2, mixed)
        late[3].wait_recv()
        prod[:, :COLS] = dot(rows, wco[...])
        prod[:, COLS:] = dot(rows, far_wco[...])
        head_sums(1, core_s2, core_r2, ys2, yr2, delta2)

    with jax.named_scope("pair_columns"):
        last_s[...] = summed[...].astype(BF16)
        copy = pair_copy(9, last_s, last_r, pair_peer)
        begin(copy)
        for dz in range(NZ):
            for t in range(2):
                rows = slice(dz * BLK + t * RB, dz * BLK + (t + 1) * RB)
                out[t, rows_at(0, dz), :] = hid[rows, :COLS]
        copy.wait_recv()
        for dz in range(NZ):
            for t in range(2):
                rows = slice(dz * BLK + t * RB, dz * BLK + (t + 1) * RB)
                out[t, rows_at(1, dz), :] = far_hid[rows, :] + last_r[rows, :].astype(F32)
    for copy in pending:
        copy.wait_send()


def body(
    hidden_in, norm_gains, w_qkv, w_self_out, w_cross_q, w_cross_out, pos_bias, self_cache, memory, parents
):
    dma = pltpu.SemaphoreType.DMA
    wide1, wide2 = 3 * INNER + LANES, INNER + LANES
    half_pair = [pltpu.VMEM((HALF, WIDE), BF16)] * 2
    quarters = [pltpu.VMEM((NY - 1, HALF // NY, WIDE), BF16)] * 2
    head_buffers = [*half_pair, *quarters, pltpu.VMEM((2, NY, HALF // NY, WIDE), BF16)]
    in_vmem = pl.BlockSpec(memory_space=pltpu.VMEM)
    hidden_out, cache_rows = pl.pallas_call(
        kernel,
        out_shape=(
            jax.ShapeDtypeStruct(hidden_in.shape, F32),
            jax.ShapeDtypeStruct((2, RB * (PREV + 2), INNER), BF16),
        ),
        in_specs=[in_vmem] * 10,
        out_specs=(in_vmem, in_vmem),
        scratch_shapes=[
            pltpu.VMEM((ROWS, COLS), F32),
            pltpu.VMEM((ROWS, COLS), F32),
            pltpu.VMEM((8, COLS), F32),
            pltpu.VMEM((8, COLS), F32),
            pltpu.VMEM((3, COLS, INNER), BF16),
            pltpu.VMEM(w_self_out.shape, BF16),
            pltpu.VMEM(w_cross_q.shape, BF16),
            pltpu.VMEM(w_cross_out.shape, BF16),
            pltpu.VMEM(memory.shape, BF16),
            pltpu.VMEM((ROWS, WIDE), F32),
            pltpu.VMEM((ROWS, COLS), F32),
            pltpu.VMEM((ROWS, WIDE), F32),
            *[pltpu.VMEM((NZ - 1, BLK, wide1), BF16)] * 2,
            pltpu.VMEM((ROWS, wide1), F32),
            *[pltpu.VMEM((NZ - 1, BLK, wide2), BF16)] * 2,
            pltpu.VMEM((ROWS, wide2), F32),
            *[pltpu.VMEM((NZ - 1, BLK, wide2), BF16)] * 2,
            *[pltpu.VMEM((2, NALL, SLOTS * CP, COLS), BF16)] * 2,
            *[pltpu.VMEM((NALL, SLOTS * KP, LANES), BF16)] * 2,
            *[pltpu.VMEM((NZ, BLK, INNER), BF16)] * 3,
            *[pltpu.VMEM((ROWS, COLS), BF16)] * 2,
            *head_buffers,
            *head_buffers,
            dma((10,)), dma((10,)), dma((3, NZ - 1)), dma((3, NZ - 1)),
            dma((2, NALL)), dma((2, NALL)), dma((NALL,)), dma((NALL,)),
            dma((3, NZ)), dma((3, NZ)),
            dma((2,)), dma((2,)), dma((2, NY - 1)), dma((2, NY - 1)),
            dma((2, NY)), dma((2, NY)), dma((2, NY)), dma((2, NY)),
        ],
        compiler_params=pltpu.CompilerParams(
            collective_id=0, has_side_effects=True, vmem_limit_bytes=58 * 1024 * 1024
        ),
        name="decode",
    )(
        hidden_in, norm_gains, w_qkv.transpose(1, 0, 2), w_self_out, w_cross_q, w_cross_out, pos_bias.T,
        self_cache[:, 0].transpose(0, 2, 1, 3), memory, parents.reshape(2, NALL, RB),
    )
    return hidden_out, cache_rows.reshape(2, 1, RB, PREV + 2, INNER)


def solution(mesh):
    placed = (
        P(None, "beam", "blk"),
        P(None, "blk"),
        P("blk", None, "head"),
        P("head", "blk"),
        P("blk", "head"),
        P("head", "blk"),
        P("head", None),
        P(None, "beam", "blk", None, "head"),
        P(None, "blk", "head"),
        P(),
    )
    return jax.shard_map(
        body,
        mesh=mesh,
        in_specs=placed,
        out_specs=(P(None, "beam", "blk"), P(None, "beam", "blk", None, "head")),
        check_vma=False,
    )
```

time: 721 us -> 158 us (0.22)
  waiting for transfers between devices: 362 us -> 0 us
  blocking collectives: 236 us -> 0 us
  Pallas kernels: 0 us -> 152 us
  local copies, waits for them, and re-layouts: 49.8 us -> 4.67 us
  other arithmetic: 24.3 us -> 0 us
  starting transfers between devices: 17.8 us -> 0 us
  between operations: 14.9 us -> 0.66 us
  matrix products: 13.2 us -> 0 us
    psum x4 -> x0, waiting for transfers between devices: 335 us -> none  [the longest x2 185 us: project(): summed, square_sum = lax.psum((partial_sum, squares), 'blk')]
    all_gather x6 -> x0, blocking collectives: 159 us -> none  [the longest x4 101 us: combined_all(): lax.all_gather(a.astype(kind), axis)]
    pallas_call x0 -> x1, Pallas kernels: none -> 152 us  [body(): pl.pallas_call(kernel, out_shape=(jax.ShapeDtypeStruct(hidden_in.shape, F...]
    psum x2 -> x0, blocking collectives: 76.6 us -> none  [project(): summed, square_sum = lax.psum((partial_sum, squares), 'blk')]
    dynamic_slice x62 -> x0, local copies, waits for them, and re-layouts: 33.4 us -> none  [the longest x60 33.3 us: take(): lax.dynamic_index_in_dim(a, source, 0, False).astype(own.dtype)]
    all_gather x2 -> x0, waiting for transfers between devices: 27 us -> none  [combined_all(): lax.all_gather(a.astype(kind), axis)]
    all_to_all x2 -> x0, starting transfers between devices: 17.3 us -> none  [reorder(): lax.all_to_all(outgoing, ('blk', 'beam'), split_axis=1, concat_axis=1, ti...]
    dot_general x16 -> x0, matrix products: 13.2 us -> none  [the longest x4 7.11 us: project(): partial_sum = jnp.dot(normed, weight, preferred_element_type=jnp.float32)]
  transfers between devices with their start and end apart: 8 -> 0, of which waited for: 5 -> 0; matrix products, arithmetic and copies ran while one was open for 5% -> 0% of each run, Pallas kernels for 0% -> 0%
where the time goes in v2:
time: 158 us; the launch traced here: 157 us
  Pallas kernels  152 us (96%)
  local copies, waits for them, and re-layouts  4.67 us (3%)
    pallas_call x1, Pallas kernels, body(): pl.pallas_call(kernel, out_shape=(jax.ShapeDtypeStruct(hidden_in.shape, F...  152 us
    unnamed x7, local copies, waits for them, and re-layouts  3.97 us

profile of v2, /device:TPU:1, one launch (start us, length us, event | category | flops | bytes accessed | tf_op | source)
XLA Modules:
  0.0 157.5 jit_solution(6582138535211754431)
XLA Ops:
  0.6 0.0 copy-start.1
  0.6 1.4 copy.14
  2.0 0.0 copy-done.1
  2.0 0.7 reshape.10.parents
  2.7 152.1 %decode.1 = (f32[2,256,256]{2,1,0:T(8,128)}, bf16[2,128,512]{2,1,0:T(8,128)(2,1)}) custom-call(f32[2,256,256]{2,1,0:T(8,128)} %hidden.1, f32[2,256]{1,0:T(2,128)} %gains.1, bf16[3,256,512]{2,1,0:T(8,128)(2,1)} %bitcast.8, bf16[512,256]{1,0:T(8,128)(2,1)} %wso.1, bf16[256,512]{1,0:T(8,128)(2,1)} %wcq.1, bf16[512,256]{1,0:T(8,128)(2,1)} %wco.1, ...), custom_call_target="tpu_custom_call" | custom-call | tf_op jit(solution)/shard_map/decode/pallas_call | solution.py:537
  154.8 0.0 copy-start
  154.8 1.9 %copy.18 = f32[2,256,256]{2,1,0:T(8,128)} copy(f32[2,256,256]{2,1,0:T(8,128)} %get-tuple-element.12) | data formatting | bytes 1048576
  156.8 0.0 copy-done
  156.8 0.7 copy.19
Async XLA Ops:
  0.6 1.4 copy-start.1
  154.8 1.9 %copy-start = (bf16[2,128,512]{2,1,0:T(8,128)(2,1)S(1)}, bf16[2,128,512]{2,1,0:T(8,128)(2,1)}, u32[]{:S(2)}) copy-start(bf16[2,128,512]{2,1,0:T(8,128)(2,1)} %get-tuple-element.5) | copy-start | bytes 786436

commit v3 on v2

--- a/solution.py
+++ b/solution.py
@@ -93,14 +93,51 @@
     return jnp.where(piece_mask((rows, cols), 1, pieces), full, 0.0).astype(BF16)
 
 
+def piece_rows(p):
+    q = iota((NALL * SLOTS, NALL * SLOTS * KP), 0)
+    row = ((q & (NALL - 1)) * SLOTS + (q >> 5)) * KP + p
+    return jnp.where(iota(q.shape, 1) == row, 1.0, 0.0).astype(BF16)
+
+
+def head_codes(four):
+    group = (iota(four[0].shape, 1) >> 4) & 3
+    low_pair, high_pair = jnp.where(group == 0, four[0], four[1]), jnp.where(group == 2, four[2], four[3])
+    return encode(jnp.where(group < 2, low_pair, high_pair))
+
+
+def attend(q, keys, values, biases, ones):
+    rows = q.shape[0]
+    products = jnp.concatenate([q * k.astype(F32) for k in keys], axis=0)
+    high = products.astype(BF16)
+    low = (products - high.astype(F32)).astype(BF16)
+    sums = dot(high, ones) + dot(low, ones)
+    scores = [sums[j * rows : (j + 1) * rows] + b for j, b in enumerate(biases)]
+    peak = scores[0]
+    for s in scores[1:]:
+        peak = jnp.maximum(peak, s)
+    weights = [jnp.exp(s - peak) for s in scores]
+    whole, acc = weights[0], weights[0].astype(BF16).astype(F32) * values[0].astype(F32)
+    for w, v in zip(weights[1:], values[1:]):
+        whole += w
+        acc += w.astype(BF16).astype(F32) * v.astype(F32)
+    return acc, peak, whole
+
+
 def picks(parents, x, z, beam):
     square = (NALL, NALL)
     o, block = iota(square, 0), iota(square, 1)
     flip_x, flip_b = (o >> 3) & 1, o >> 4
     at_offset = (beam + flip_b - 2 * beam * flip_b) * NBLK + (x + flip_x - 2 * x * flip_x) * NZ + ((z + o) & 7)
     permute = jnp.where(at_offset == block, 1.0, 0.0).astype(BF16)
-    source = dot(permute, (parents >> 4).astype(F32).astype(BF16))
-    local = dot(permute, (parents & 15).astype(F32).astype(BF16))
+    wide = (NALL, NALL * RB)
+    in_block = (iota(wide, 1) >> 4) == iota(wide, 0)
+    fold = jnp.where((iota(wide[::-1][:1] + (RB,), 0) & 15) == iota(wide[::-1][:1] + (RB,), 1), 1.0, 0.0).astype(BF16)
+
+    def folded(row):
+        blocks = dot(jnp.where(in_block, row.astype(F32), 0.0).astype(BF16), fold)
+        return dot(permute, blocks.astype(BF16))
+
+    source, local = folded(parents >> 4), folded(parents & 15)
     lane = iota((NALL, RB), 1)
     slot = jnp.zeros((NALL, RB), F32)
     for k in range(RB - 1):
@@ -120,14 +157,15 @@
 
 
 def kernel(
-    hidden, gains, wqkv, wso, wcq, wco, bias, cache, memory, parents,
+    hidden, gains, wqkv_hbm, wso_hbm, wcq_hbm, wco_hbm, bias, cache, memory_hbm, parents,
     out, cache_out,
+    wqkv, wso, wcq, wco, memory,
     far_hid, near_hid, far_gain, near_gain, far_wqkv, far_wso, far_wcq, far_wco, far_memory,
     hid, summed, prod, zs1, zr1, own1, zs2, zr2, own2, zs3, zr3,
-    hop_send, hop_recv, kv_send, kv_recv, att, query, mixed, last_s, last_r,
+    hop_send, hop_recv, kv_send, kv_recv, ask_send, ask_recv, reply_send, reply_recv, att, query, mixed, last_s, last_r,
     core_s, core_r, ys, yr, delta, core_s2, core_r2, ys2, yr2, delta2,
     sem_ws, sem_wr, sem_zs, sem_zr, sem_hs, sem_hr, sem_ks, sem_kr, sem_gs, sem_gr,
-    sem_cs, sem_cr, sem_ys, sem_yr, sem_ds, sem_dr, sem_es, sem_er,
+    sem_cs, sem_cr, sem_ys, sem_yr, sem_ds, sem_dr, sem_es, sem_er, sem_as, sem_ar, sem_rs, sem_rr, sem_in,
 ):
     blk, beam, head = lax.axis_index("blk"), lax.axis_index("beam"), lax.axis_index("head")
     x, z = blk // NZ, lax.rem(blk, NZ)
@@ -141,6 +179,12 @@
 
     def all_peer(o):
         where = {"blk": block_at((o // NZ) % NX, o % NZ)}
+        if o >= NBLK:
+            where["beam"] = 1 - beam
+        return where
+
+    def back_peer(o):
+        where = {"blk": block_at((o // NZ) % NX, (NZ - o) % NZ)}
         if o >= NBLK:
             where["beam"] = 1 - beam
         return where
@@ -166,6 +210,14 @@
         peers += [core_peer] + [y_peer(dy) for dy in range(1, NY)]
         for peer in peers:
             pl.semaphore_signal(barrier, inc=1, device_id=peer, device_id_type=MESH)
+        inward = [
+            pltpu.make_async_copy(src, dst, sem_in.at[i])
+            for i, (src, dst) in enumerate(
+                ((wqkv_hbm, wqkv), (wso_hbm, wso), (wcq_hbm, wcq), (memory_hbm, memory), (wco_hbm, wco))
+            )
+        ]
+        for copy in inward:
+            copy.start()
         for dz in range(NZ):
             for t in range(2):
                 rows = slice(dz * BLK + t * RB, dz * BLK + (t + 1) * RB)
@@ -173,6 +225,15 @@
                 hid[rows, :COLS] = hidden[t, rows_at(0, dz), :]
         far_gain[...] = jnp.zeros_like(far_gain)
         far_gain[:2, :] = gains[...]
+
+    with jax.named_scope("own_products"):
+        send0, recv0 = picks(parents[0:1, :], x, z, beam)
+        pieces = [
+            cache[kv, pos, :, c * COLS : (c + 1) * COLS] for kv in range(2) for pos in range(PREV) for c in range(2)
+        ]
+        picked = dot(spread_matrix(send0, CP), jnp.concatenate(pieces, axis=0)).astype(BF16)
+        hop_send[0] = picked.reshape(NALL, SLOTS * CP, COLS)
+        hop_recv[0, 0] = hop_send[0, 0]
         pl.semaphore_wait(barrier, len(peers))
 
     pending = []
@@ -190,14 +251,14 @@
     early = [
         pair_copy(0, far_hid.at[my_half], near_hid.at[my_half], pair_peer),
         pair_copy(1, far_gain, near_gain, pair_peer),
-        pair_copy(2, wqkv.at[:, pl.ds(0, SPLIT)], far_wqkv.at[:, pl.ds(0, SPLIT)], other_peer),
-        pair_copy(3, wqkv.at[:, pl.ds(SPLIT, COLS - SPLIT)], far_wqkv.at[:, pl.ds(SPLIT, COLS - SPLIT)], pair_peer),
+        pair_copy(2, wqkv_hbm.at[:, pl.ds(0, SPLIT)], far_wqkv.at[:, pl.ds(0, SPLIT)], other_peer),
+        pair_copy(3, wqkv_hbm.at[:, pl.ds(SPLIT, COLS - SPLIT)], far_wqkv.at[:, pl.ds(SPLIT, COLS - SPLIT)], pair_peer),
     ]
     late = [
-        pair_copy(4, wso, far_wso, other_peer),
-        pair_copy(5, wcq, far_wcq, pair_peer),
-        pair_copy(6, memory, far_memory, other_peer),
-        pair_copy(7, wco, far_wco, pair_peer),
+        pair_copy(4, wso_hbm, far_wso, other_peer),
+        pair_copy(5, wcq_hbm, far_wcq, pair_peer),
+        pair_copy(6, memory_hbm, far_memory, other_peer),
+        pair_copy(7, wco_hbm, far_wco, pair_peer),
     ]
     for copy in early:
         begin(copy)
@@ -206,13 +267,6 @@
         return remote(
             hop_send.at[step, o], hop_recv.at[step, o], sem_hs.at[step, o], sem_hr.at[step, o], all_peer(o)
         )
-
-    def hop_start(step, chosen, rows):
-        picked = dot(spread_matrix(chosen, CP), rows).astype(BF16)
-        hop_send[step] = picked.reshape(NALL, SLOTS * CP, COLS)
-        hop_recv[step, 0] = hop_send[step, 0]
-        for o in range(1, NALL):
-            begin(hop_copy(step, o))
 
     def hop_end(step, chosen):
         pick = gather_matrix(chosen, CP)
@@ -221,14 +275,10 @@
         return dot(pick, hop_recv[step].reshape(NALL * SLOTS * CP, COLS)).astype(BF16)
 
     with jax.named_scope("cache_send"):
-        send0, recv0 = picks(parents[0], x, z, beam)
-        pieces = [
-            cache[kv, pos, :, c * COLS : (c + 1) * COLS] for kv in range(2) for pos in range(PREV) for c in range(2)
-        ]
-        hop_start(0, send0, jnp.concatenate(pieces, axis=0))
+        for o in range(1, NALL):
+            begin(hop_copy(0, o))
         for copy in late:
             begin(copy)
-        send1, recv1 = picks(parents[1], x, z, beam)
 
     def z_copy(phase, zs, zr, dz):
         return remote(
@@ -254,7 +304,7 @@
     def square_sums(states):
         return jnp.broadcast_to(jnp.sum(states * states, axis=1, keepdims=True), (ROWS, LANES))
 
-    def gather_rows(phase, blocks):
+    def gather_rows(phase, blocks, meanwhile=None):
         def copy(dz):
             back = NZ - dz
             return remote(
@@ -263,6 +313,8 @@
 
         for dz in far_first:
             begin(copy(dz))
+        if meanwhile:
+            meanwhile()
         for dz in far_first[::-1]:
             remote(
                 blocks.at[0], blocks.at[dz], sem_gs.at[phase, dz], sem_gr.at[phase, dz], z_peer(dz)
@@ -275,7 +327,7 @@
         start = half * HALF + lax.rem(y + dy, NY) * quarter
         return pl.ds(pl.multiple_of(start, quarter), quarter)
 
-    def head_sums(phase, core_s, core_r, ys, yr, delta):
+    def head_sums(phase, core_s, core_r, ys, yr, delta, meanwhile=None):
         core_s[...] = prod[its_half, :].astype(BF16)
         copy = remote(core_s, core_r, sem_cs.at[phase], sem_cr.at[phase], core_peer)
         begin(copy)
@@ -291,6 +343,8 @@
         for dy in order:
             ys[dy - 1] = prod[quarter_rows(core, dy), :].astype(BF16)
             begin(copy_sum(dy))
+        if meanwhile:
+            meanwhile()
         total = prod[quarter_rows(core, 0), :]
         for dy in (1, 3, 2):
             copy_sum(dy).wait_recv()
@@ -322,16 +376,17 @@
             half = core if part == 0 else 1 - core
             for dy in range(NY):
                 added = delta[part, dy].astype(F32)
-                hid[quarter_rows(half, dy), :] += added
                 if phase == 0:
-                    summed[quarter_rows(half, dy), :] = added[:, COLS:]
+                    hid[quarter_rows(half, dy), :] += added
+                    summed[quarter_rows(half, dy), :] = added
                 else:
-                    summed[quarter_rows(half, dy), :] += added[:, COLS:]
+                    summed[quarter_rows(half, dy), :] += added
 
     with jax.named_scope("qkv_products"):
         width1 = 3 * INNER
         states = hid[:, :COLS]
         normed = (states * gains[0:1, :]).astype(BF16)
+        inward[0].wait()
         for j in range(3):
             own1[:, j * INNER : (j + 1) * INNER] = dot(normed, wqkv[j])
         own1[:, width1:] = square_sums(states)
@@ -353,80 +408,132 @@
         total, scale = scatter_sums(0, width1, zs1, zr1, own1)
         qkv = (total * scale).astype(BF16)
 
-    with jax.named_scope("cache_forward"):
-        held0 = hop_end(0, recv0)
-        hop_start(1, send1, held0)
+    def ask_copy(o):
+        return remote(ask_send.at[o], ask_recv.at[o], sem_as.at[o], sem_ar.at[o], back_peer(o))
+
+    def reply_copy(o):
+        return remote(reply_send.at[o], reply_recv.at[o], sem_rs.at[o], sem_rr.at[o], all_peer(o))
 
     def kv_copy(o):
         return remote(kv_send.at[o], kv_recv.at[o], sem_ks.at[o], sem_kr.at[o], all_peer(o))
 
-    with jax.named_scope("entry_send"):
-        fresh = qkv[:RB, INNER:]
-        stacked = jnp.concatenate([fresh[:, p * LANES : (p + 1) * LANES] for p in range(KP)], axis=0)
-        kv_send[...] = dot(spread_matrix(send1, KP), stacked).astype(BF16).reshape(NALL, SLOTS * KP, LANES)
-        kv_recv[0] = kv_send[0]
-        for o in range(1, NALL):
-            begin(kv_copy(o))
-
-    with jax.named_scope("cache_last"):
-        held1 = hop_end(1, recv1)
-
-    with jax.named_scope("entry_receive"):
-        pick = gather_matrix(recv1, KP)
-        for o in range(1, NALL):
-            kv_copy(o).wait_recv()
-        moved = dot(pick, kv_recv[...].reshape(NALL * SLOTS * KP, LANES)).astype(BF16)
-
     def side_by_side(rows, first, count):
         return jnp.concatenate([rows[(first + p) * RB : (first + p + 1) * RB] for p in range(count)], axis=1)
 
-    with jax.named_scope("self_attention"):
-        grown = []
-        for t, held in enumerate((held0, held1)):
-            sides = []
-            for kv in range(2):
-                side = [side_by_side(held, (kv * PREV + pos) * 2, 2) for pos in range(PREV)]
-                if t == 1:
-                    side.append(side_by_side(moved, kv * KP // 2, KP // 2))
-                side.append(qkv[t * RB : (t + 1) * RB, (1 + kv) * INNER : (2 + kv) * INNER])
-                sides.append(side)
-            grown.append(sides)
+    def stacked(rows):
+        return [rows[:, p * LANES : (p + 1) * LANES] for p in range(rows.shape[1] // LANES)]
+
+    def entry(t, kv):
+        return qkv[t * RB : (t + 1) * RB, (1 + kv) * INNER : (2 + kv) * INNER]
+
+    messages = (NALL, SLOTS * KP, LANES)
+    flat = (NALL * SLOTS * KP, LANES)
+    queries_of = [
+        (qkv[t * RB : (t + 1) * RB, :INNER].astype(F32) * 0.125).astype(BF16) for t in range(2)
+    ]
+    with jax.named_scope("query_send"):
+        send1, recv1 = picks(parents[1:2, :], x, z, beam)
+        four = stacked(queries_of[1])
+        asked = jnp.concatenate(four + four, axis=0)
+        ask_send[...] = dot(spread_matrix(recv1, KP), asked).astype(BF16).reshape(messages)
+        ask_recv[0] = ask_send[0]
+        for o in range(1, NALL):
+            begin(ask_copy(o))
+
+    with jax.named_scope("parent_attention"):
         same_head = (iota((INNER, INNER), 0) >> 6) == (iota((INNER, INNER), 1) >> 6)
         ones = jnp.where(same_head, 1.0, 0.0).astype(BF16)
         of_head = jnp.where((iota((8, INNER), 1) >> 6) == iota((8, INNER), 0), 1.0, 0.0).astype(BF16)
-        wide_bias = sum(dot(part.astype(BF16), of_head) for part in split3(bias[...]))
-        for t in range(2):
-            keys, values = grown[t]
-            q = qkv[t * RB : (t + 1) * RB, :INNER].astype(F32) * 0.125
-            products = jnp.concatenate([q * k.astype(F32) for k in keys], axis=0)
-            high = products.astype(BF16)
-            low = (products - high.astype(F32)).astype(BF16)
-            sums = dot(high, ones) + dot(low, ones)
-            last = PREV + t
-            scores = [
-                sums[j * RB : (j + 1) * RB] + wide_bias[last - j : last - j + 1, :] for j in range(last + 1)
-            ]
-            peak = scores[0]
-            for s in scores[1:]:
-                peak = jnp.maximum(peak, s)
-            weights = [jnp.exp(s - peak) for s in scores]
-            whole, acc = weights[0], weights[0].astype(BF16).astype(F32) * values[0].astype(F32)
-            for w, v in zip(weights[1:], values[1:]):
-                whole += w
-                acc += w.astype(BF16).astype(F32) * v.astype(F32)
-            att[0, t * RB : (t + 1) * RB, :] = (acc / whole).astype(BF16)
+        wide_bias = sum(
+            lax.dot_general(part.astype(BF16), of_head, (((0,), (0,)), ((), ())), preferred_element_type=F32)
+            for part in split3(bias[...])
+        )
+        held0 = hop_end(0, recv0)
+        grown0 = [
+            [side_by_side(held0, (kv * PREV + pos) * 2, 2) for pos in range(PREV)] + [entry(0, kv)] for kv in range(2)
+        ]
+        copies = [[dot(send1, rows) for rows in side] for side in grown0]
+        rows_of_piece = [piece_rows(p) for p in range(5)]
+        back = jnp.concatenate(rows_of_piece, axis=0)
+        for o in range(1, NALL):
+            ask_copy(o).wait_recv()
+        arrived = ask_recv[...].reshape(flat)
+        q = jnp.concatenate([dot(rows_of_piece[p], arrived) for p in range(4)], axis=1)
+        last = PREV + 1
+        acc, peak, whole = attend(
+            q, *copies, [wide_bias[last - j : last - j + 1, :] for j in range(last)], ones
+        )
+        mine = (acc / whole).astype(BF16)
+        lse = peak + jnp.log(whole)
+        code = head_codes(stacked(lse))
+        turned = lax.dot_general(
+            back, jnp.concatenate(stacked(mine) + [code], axis=0), (((0,), (0,)), ((), ())), preferred_element_type=F32
+        )
+        reply_send[...] = turned.astype(BF16).reshape(messages)
+        reply_recv[0] = reply_send[0]
+        for o in range(1, NALL):
+            begin(reply_copy(o))
+
+    with jax.named_scope("self_attention"):
+        acc, _, whole = attend(
+            queries_of[0].astype(F32), *grown0,
+            [wide_bias[PREV - j : PREV - j + 1, :] for j in range(PREV + 1)], ones,
+        )
+        att[0, :RB, :] = (acc / whole).astype(BF16)
+        pick1 = gather_matrix(recv1, KP)
+        spread_heads = decode_heads()
+        fresh = queries_of[1].astype(F32) * entry(1, 0).astype(F32)
+        high = fresh.astype(BF16)
+        low = (fresh - high.astype(F32)).astype(BF16)
+        score = dot(high, ones) + dot(low, ones) + wide_bias[0:1, :]
+        for o in range(1, NALL):
+            reply_copy(o).wait_recv()
+        replies = dot(pick1, reply_recv[...].reshape(flat)).astype(BF16)
+        lse = dot(replies[4 * RB : 5 * RB], spread_heads)
+        peak = jnp.maximum(lse, score)
+        w_old, w_new = jnp.exp(lse - peak), jnp.exp(score - peak)
+        acc = side_by_side(replies, 0, 4).astype(F32) * w_old + w_new * entry(1, 1).astype(F32)
+        att[0, RB:, :] = (acc / (w_old + w_new)).astype(BF16)
+
+    def cache_ready():
+        picked = dot(spread_matrix(send1, CP), held0).astype(BF16)
+        hop_send[1] = picked.reshape(NALL, SLOTS * CP, COLS)
+        hop_recv[1, 0] = hop_send[1, 0]
+        added = jnp.concatenate(stacked(entry(0, 0)) + stacked(entry(0, 1)), axis=0)
+        kv_send[...] = dot(spread_matrix(send1, KP), added).astype(BF16).reshape(messages)
+        kv_recv[0] = kv_send[0]
+
+    def cache_start():
+        for o in range(1, NALL):
+            begin(hop_copy(1, o))
+            begin(kv_copy(o))
+
+    def cache_end():
+        held1 = hop_end(1, recv1)
+        for o in range(1, NALL):
+            kv_copy(o).wait_recv()
+        moved = dot(pick1, kv_recv[...].reshape(flat)).astype(BF16)
+        place = iota((RB * (PREV + 2), RB * (PREV + 2)), 0)
+        from_row = (place & 7) * RB + (place >> 3)
+        turn = jnp.where(from_row == iota(place.shape, 1), 1.0, 0.0).astype(BF16)
+        for kv in range(2):
+            side = [side_by_side(held1, (kv * PREV + pos) * 2, 2) for pos in range(PREV)]
+            side += [side_by_side(moved, kv * KP // 2, KP // 2), entry(1, kv)]
+            cache_out[kv] = dot(turn, jnp.concatenate(side, axis=0)).astype(BF16)
 
     with jax.named_scope("self_out"):
-        rows = gather_rows(0, att)
+        rows = gather_rows(0, att, cache_ready)
+        inward[1].wait()
         late[0].wait_recv()
         prod[:, :COLS] = dot(rows, wso[...])
         prod[:, COLS:] = dot(rows, far_wso[...])
-        head_sums(0, core_s, core_r, ys, yr, delta)
+        head_sums(0, core_s, core_r, ys, yr, delta, cache_start)
 
     with jax.named_scope("cross_query_products"):
         states = hid[...]
         gain = jnp.concatenate([gains[1:2, :], near_gain[1:2, :]], axis=1)
         normed = (states * gain).astype(BF16)
+        inward[2].wait()
         late[1].wait_recv()
         own2[:, :INNER] = dot(normed[:, :COLS], wcq[...]) + dot(normed[:, COLS:], far_wcq[...])
         own2[:, INNER:] = square_sums(states)
@@ -436,14 +543,10 @@
         query[0] = ((total * scale).astype(BF16).astype(F32) * 0.125).astype(BF16)
 
     with jax.named_scope("cross_query_gather"):
-        place = iota((RB * (PREV + 2), RB * (PREV + 2)), 0)
-        from_row = (place & 7) * RB + (place >> 3)
-        turn = jnp.where(from_row == iota(place.shape, 1), 1.0, 0.0).astype(BF16)
         queries = gather_rows(1, query)
-        for kv in range(2):
-            cache_out[kv] = dot(turn, jnp.concatenate(grown[1][kv], axis=0)).astype(BF16)
 
     with jax.named_scope("cross_partial"):
+        inward[3].wait()
         late[2].wait_recv()
         tokens = 2 * memory.shape[1]
         low_lane = iota((tokens, LANES), 1) < 64
@@ -477,16 +580,13 @@
             narrow = acc.astype(BF16)
             for dz in range(1, NZ):
                 zs3[dz - 1, :, cols] = narrow[dz * BLK : (dz + 1) * BLK]
-        group = (iota((ROWS, LANES), 1) >> 4) & 3
-        low_pair, high_pair = jnp.where(group == 0, lses[0], lses[1]), jnp.where(group == 2, lses[2], lses[3])
-        code = encode(jnp.where(group < 2, low_pair, high_pair))
+        code = head_codes(lses)
         for dz in range(1, NZ):
             zs3[dz - 1, :, INNER:] = code[dz * BLK : (dz + 1) * BLK]
 
     with jax.named_scope("cross_join"):
         for dz in far_first:
             begin(z_copy(2, zs3, zr3, dz))
-        spread_heads = decode_heads()
         peak = jnp.concatenate([lse[:BLK] for lse in lses], axis=1)
         parts = [(jnp.concatenate(accs, axis=1), peak)]
         for dz in far_first[::-1]:
@@ -502,25 +602,26 @@
         mixed[0] = (acc / whole).astype(BF16)
 
     with jax.named_scope("cross_out"):
-        rows = gather_rows(2, mixed)
+        rows = gather_rows(2, mixed, cache_end)
+        inward[4].wait()
         late[3].wait_recv()
         prod[:, :COLS] = dot(rows, wco[...])
         prod[:, COLS:] = dot(rows, far_wco[...])
         head_sums(1, core_s2, core_r2, ys2, yr2, delta2)
 
     with jax.named_scope("pair_columns"):
-        last_s[...] = summed[...].astype(BF16)
+        last_s[...] = summed[:, COLS:].astype(BF16)
         copy = pair_copy(9, last_s, last_r, pair_peer)
         begin(copy)
         for dz in range(NZ):
             for t in range(2):
                 rows = slice(dz * BLK + t * RB, dz * BLK + (t + 1) * RB)
-                out[t, rows_at(0, dz), :] = hid[rows, :COLS]
+                out[t, rows_at(0, dz), :] = summed[rows, :COLS]
         copy.wait_recv()
         for dz in range(NZ):
             for t in range(2):
                 rows = slice(dz * BLK + t * RB, dz * BLK + (t + 1) * RB)
-                out[t, rows_at(1, dz), :] = far_hid[rows, :] + last_r[rows, :].astype(F32)
+                out[t, rows_at(1, dz), :] = last_r[rows, :].astype(F32)
     for copy in pending:
         copy.wait_send()
 
@@ -534,15 +635,21 @@
     quarters = [pltpu.VMEM((NY - 1, HALF // NY, WIDE), BF16)] * 2
     head_buffers = [*half_pair, *quarters, pltpu.VMEM((2, NY, HALF // NY, WIDE), BF16)]
     in_vmem = pl.BlockSpec(memory_space=pltpu.VMEM)
-    hidden_out, cache_rows = pl.pallas_call(
+    in_hbm = pl.BlockSpec(memory_space=pl.ANY)
+    added, cache_rows = pl.pallas_call(
         kernel,
         out_shape=(
             jax.ShapeDtypeStruct(hidden_in.shape, F32),
             jax.ShapeDtypeStruct((2, RB * (PREV + 2), INNER), BF16),
         ),
-        in_specs=[in_vmem] * 10,
+        in_specs=[in_vmem] * 2 + [in_hbm] * 4 + [in_vmem] * 2 + [in_hbm, in_vmem],
         out_specs=(in_vmem, in_vmem),
         scratch_shapes=[
+            pltpu.VMEM((3, COLS, INNER), BF16),
+            pltpu.VMEM(w_self_out.shape, BF16),
+            pltpu.VMEM(w_cross_q.shape, BF16),
+            pltpu.VMEM(w_cross_out.shape, BF16),
+            pltpu.VMEM(memory.shape, BF16),
             pltpu.VMEM((ROWS, COLS), F32),
             pltpu.VMEM((ROWS, COLS), F32),
             pltpu.VMEM((8, COLS), F32),
@@ -552,16 +659,14 @@
             pltpu.VMEM(w_cross_q.shape, BF16),
             pltpu.VMEM(w_cross_out.shape, BF16),
             pltpu.VMEM(memory.shape, BF16),
-            pltpu.VMEM((ROWS, WIDE), F32),
-            pltpu.VMEM((ROWS, COLS), F32),
-            pltpu.VMEM((ROWS, WIDE), F32),
+            *[pltpu.VMEM((ROWS, WIDE), F32)] * 3,
             *[pltpu.VMEM((NZ - 1, BLK, wide1), BF16)] * 2,
             pltpu.VMEM((ROWS, wide1), F32),
             *[pltpu.VMEM((NZ - 1, BLK, wide2), BF16)] * 2,
             pltpu.VMEM((ROWS, wide2), F32),
             *[pltpu.VMEM((NZ - 1, BLK, wide2), BF16)] * 2,
             *[pltpu.VMEM((2, NALL, SLOTS * CP, COLS), BF16)] * 2,
-            *[pltpu.VMEM((NALL, SLOTS * KP, LANES), BF16)] * 2,
+            *[pltpu.VMEM((NALL, SLOTS * KP, LANES), BF16)] * 6,
             *[pltpu.VMEM((NZ, BLK, INNER), BF16)] * 3,
             *[pltpu.VMEM((ROWS, COLS), BF16)] * 2,
             *head_buffers,
@@ -571,16 +676,17 @@
             dma((3, NZ)), dma((3, NZ)),
             dma((2,)), dma((2,)), dma((2, NY - 1)), dma((2, NY - 1)),
             dma((2, NY)), dma((2, NY)), dma((2, NY)), dma((2, NY)),
+            dma((NALL,)), dma((NALL,)), dma((NALL,)), dma((NALL,)), dma((5,)),
         ],
         compiler_params=pltpu.CompilerParams(
             collective_id=0, has_side_effects=True, vmem_limit_bytes=58 * 1024 * 1024
         ),
         name="decode",
     )(
-        hidden_in, norm_gains, w_qkv.transpose(1, 0, 2), w_self_out, w_cross_q, w_cross_out, pos_bias.T,
-        self_cache[:, 0].transpose(0, 2, 1, 3), memory, parents.reshape(2, NALL, RB),
+        hidden_in, norm_gains, w_qkv.transpose(1, 0, 2), w_self_out, w_cross_q, w_cross_out, pos_bias,
+        self_cache[:, 0].transpose(0, 2, 1, 3), memory, parents,
     )
-    return hidden_out, cache_rows.reshape(2, 1, RB, PREV + 2, INNER)
+    return hidden_in + added, cache_rows.reshape(2, 1, RB, PREV + 2, INNER)
 
 
 def solution(mesh):

time: 158 us -> 156 us (0.987)
  local copies, waits for them, and re-layouts: 4.67 us -> 0.71 us
  other arithmetic: 0 us -> 1.94 us
    unnamed x7 -> x5, local copies, waits for them, and re-layouts: 3.97 us -> 0.71 us
    add x0 -> x1, other arithmetic: none -> 1.94 us  [body(): return (hidden_in + added, cache_rows.reshape(2, 1, RB, PREV + 2, INNER))]
where the time goes in v3:
time: 156 us
  Pallas kernels  153 us (98%)
  other arithmetic  1.94 us (1%)
    pallas_call x1, Pallas kernels, body(): pl.pallas_call(kernel, out_shape=(jax.ShapeDtypeStruct(hidden_in.shape, F...  153 us

profile of v3, /device:TPU:1, one launch (start us, length us, event | category | flops | bytes accessed | tf_op | source)
XLA Modules:
  0.0 155.9 jit_solution(11432040944561434036)
XLA Ops:
  0.6 0.0 copy-start
  0.6 152.6 %decode.1 = (f32[2,256,256]{2,1,0:T(8,128)}, bf16[2,128,512]{2,1,0:T(8,128)(2,1)}) custom-call(f32[2,256,256]{2,1,0:T(8,128)} %hidden.1, f32[2,256]{1,0:T(2,128)} %gains.1, bf16[3,256,512]{2,1,0:T(8,128)(2,1)} %bitcast.7, bf16[512,256]{1,0:T(8,128)(2,1)} %wso_hbm.1, bf16[256,512]{1,0:T(8,128)(2,1)} %wcq_hbm.1, bf16[512,256]{1,0:T(8,128)(2,1)} %wco_hbm.1, ...), custom_call_target="tpu_custom_call" | custom-call | tf_op jit(solution)/shard_map/decode/pallas_call | solution.py:639
  153.3 0.0 copy-done
  153.3 0.0 copy-start.1
  153.3 1.9 %add.3 = f32[2,256,256]{2,1,0:T(8,128)} add(f32[2,256,256]{2,1,0:T(8,128)S(1)} %copy-done, f32[2,256,256]{2,1,0:T(8,128)} %get-tuple-element.4) | non-fusion elementwise | flops 131072 | bytes 1572864 | tf_op jit(solution)/shard_map/add | solution.py:689
  155.2 0.0 copy-done.1
  155.2 0.7 copy.14
Async XLA Ops:
  0.6 152.6 %copy-start = (f32[2,256,256]{2,1,0:T(8,128)S(1)}, f32[2,256,256]{2,1,0:T(8,128)}, u32[]{:S(2)}) copy-start(f32[2,256,256]{2,1,0:T(8,128)} %hidden.1) | copy-start | bytes 1572868
  153.3 2.0 %copy-start.1 = (bf16[2,128,512]{2,1,0:T(8,128)(2,1)S(1)}, bf16[2,128,512]{2,1,0:T(8,128)(2,1)}, u32[]{:S(2)}) copy-start(bf16[2,128,512]{2,1,0:T(8,128)(2,1)} %get-tuple-element.5) | copy-start | bytes 786436

commit v4 on v3

--- a/solution.py
+++ b/solution.py
@@ -23,6 +23,7 @@
 PREV = 6
 CP = 2 * PREV * 2
 KP = 8
+GP = 16
 LANES = 128
 SLOTS = 2
 
@@ -162,7 +163,7 @@
     wqkv, wso, wcq, wco, memory,
     far_hid, near_hid, far_gain, near_gain, far_wqkv, far_wso, far_wcq, far_wco, far_memory,
     hid, summed, prod, zs1, zr1, own1, zs2, zr2, own2, zs3, zr3,
-    hop_send, hop_recv, kv_send, kv_recv, ask_send, ask_recv, reply_send, reply_recv, att, query, mixed, last_s, last_r,
+    hop_send, hop_recv, grown_send, grown_recv, ask_send, ask_recv, reply_send, reply_recv, att, query, mixed, last_s, last_r,
     core_s, core_r, ys, yr, delta, core_s2, core_r2, ys2, yr2, delta2,
     sem_ws, sem_wr, sem_zs, sem_zr, sem_hs, sem_hr, sem_ks, sem_kr, sem_gs, sem_gr,
     sem_cs, sem_cr, sem_ys, sem_yr, sem_ds, sem_dr, sem_es, sem_er, sem_as, sem_ar, sem_rs, sem_rr, sem_in,
@@ -232,8 +233,8 @@
             cache[kv, pos, :, c * COLS : (c + 1) * COLS] for kv in range(2) for pos in range(PREV) for c in range(2)
         ]
         picked = dot(spread_matrix(send0, CP), jnp.concatenate(pieces, axis=0)).astype(BF16)
-        hop_send[0] = picked.reshape(NALL, SLOTS * CP, COLS)
-        hop_recv[0, 0] = hop_send[0, 0]
+        hop_send[...] = picked.reshape(NALL, SLOTS * CP, COLS)
+        hop_recv[0] = hop_send[0]
         pl.semaphore_wait(barrier, len(peers))
 
     pending = []
@@ -263,22 +264,12 @@
     for copy in early:
         begin(copy)
 
-    def hop_copy(step, o):
-        return remote(
-            hop_send.at[step, o], hop_recv.at[step, o], sem_hs.at[step, o], sem_hr.at[step, o], all_peer(o)
-        )
-
-    def hop_end(step, chosen):
-        pick = gather_matrix(chosen, CP)
-        for o in range(1, NALL):
-            hop_copy(step, o).wait_recv()
-        return dot(pick, hop_recv[step].reshape(NALL * SLOTS * CP, COLS)).astype(BF16)
+    def hop_copy(o):
+        return remote(hop_send.at[o], hop_recv.at[o], sem_hs.at[o], sem_hr.at[o], all_peer(o))
 
     with jax.named_scope("cache_send"):
         for o in range(1, NALL):
-            begin(hop_copy(0, o))
-        for copy in late:
-            begin(copy)
+            begin(hop_copy(o))
 
     def z_copy(phase, zs, zr, dz):
         return remote(
@@ -287,12 +278,18 @@
 
     far_first = (4, 3, 5, 2, 6, 1, 7)
 
-    def scatter_sums(phase, width, zs, zr, own):
+    def late_start():
+        for copy in late:
+            begin(copy)
+
+    def scatter_sums(phase, width, zs, zr, own, meanwhile=None):
         for dz in far_first:
             rows = slice(dz * BLK, (dz + 1) * BLK)
             zs[dz - 1, :, :width] = own[rows, :width].astype(BF16)
             zs[dz - 1, :, width:] = encode(own[rows, width:])
             begin(z_copy(phase, zs, zr, dz))
+        if meanwhile:
+            meanwhile()
         total, squares = own[:BLK, :width], own[:BLK, width:]
         for dz in far_first[::-1]:
             z_copy(phase, zs, zr, dz).wait_recv()
@@ -405,7 +402,7 @@
             own1[:, j * INNER : (j + 1) * INNER] += dot(normed, far_wqkv[j])
 
     with jax.named_scope("qkv_sums"):
-        total, scale = scatter_sums(0, width1, zs1, zr1, own1)
+        total, scale = scatter_sums(0, width1, zs1, zr1, own1, late_start)
         qkv = (total * scale).astype(BF16)
 
     def ask_copy(o):
@@ -414,8 +411,10 @@
     def reply_copy(o):
         return remote(reply_send.at[o], reply_recv.at[o], sem_rs.at[o], sem_rr.at[o], all_peer(o))
 
-    def kv_copy(o):
-        return remote(kv_send.at[o], kv_recv.at[o], sem_ks.at[o], sem_kr.at[o], all_peer(o))
+    def grown_copy(kv, o):
+        return remote(
+            grown_send.at[kv, o], grown_recv.at[kv, o], sem_ks.at[kv, o], sem_kr.at[kv, o], all_peer(o)
+        )
 
     def side_by_side(rows, first, count):
         return jnp.concatenate([rows[(first + p) * RB : (first + p + 1) * RB] for p in range(count)], axis=1)
@@ -448,7 +447,10 @@
             lax.dot_general(part.astype(BF16), of_head, (((0,), (0,)), ((), ())), preferred_element_type=F32)
             for part in split3(bias[...])
         )
-        held0 = hop_end(0, recv0)
+        pick = gather_matrix(recv0, CP)
+        for o in range(1, NALL):
+            hop_copy(o).wait_recv()
+        held0 = dot(pick, hop_recv[...].reshape(NALL * SLOTS * CP, COLS)).astype(BF16)
         grown0 = [
             [side_by_side(held0, (kv * PREV + pos) * 2, 2) for pos in range(PREV)] + [entry(0, kv)] for kv in range(2)
         ]
@@ -496,29 +498,29 @@
         att[0, RB:, :] = (acc / (w_old + w_new)).astype(BF16)
 
     def cache_ready():
-        picked = dot(spread_matrix(send1, CP), held0).astype(BF16)
-        hop_send[1] = picked.reshape(NALL, SLOTS * CP, COLS)
-        hop_recv[1, 0] = hop_send[1, 0]
-        added = jnp.concatenate(stacked(entry(0, 0)) + stacked(entry(0, 1)), axis=0)
-        kv_send[...] = dot(spread_matrix(send1, KP), added).astype(BF16).reshape(messages)
-        kv_recv[0] = kv_send[0]
-
-    def cache_start():
+        spread = spread_matrix(send1, GP)
+        for kv in range(2):
+            new = entry(0, kv)
+            halves = [new[:, :COLS], new[:, COLS:]]
+            first = kv * PREV * 2 * RB
+            rows = jnp.concatenate([held0[first : first + PREV * 2 * RB], *halves, *halves], axis=0)
+            grown_send[kv] = dot(spread, rows).astype(BF16).reshape(NALL, SLOTS * GP, COLS)
+            grown_recv[kv, 0] = grown_send[kv, 0]
+
+    def cache_start(kv):
         for o in range(1, NALL):
-            begin(hop_copy(1, o))
-            begin(kv_copy(o))
+            begin(grown_copy(kv, o))
 
     def cache_end():
-        held1 = hop_end(1, recv1)
-        for o in range(1, NALL):
-            kv_copy(o).wait_recv()
-        moved = dot(pick1, kv_recv[...].reshape(flat)).astype(BF16)
+        pick = gather_matrix(recv1, GP)
         place = iota((RB * (PREV + 2), RB * (PREV + 2)), 0)
         from_row = (place & 7) * RB + (place >> 3)
         turn = jnp.where(from_row == iota(place.shape, 1), 1.0, 0.0).astype(BF16)
         for kv in range(2):
-            side = [side_by_side(held1, (kv * PREV + pos) * 2, 2) for pos in range(PREV)]
-            side += [side_by_side(moved, kv * KP // 2, KP // 2), entry(1, kv)]
+            for o in range(1, NALL):
+                grown_copy(kv, o).wait_recv()
+            held1 = dot(pick, grown_recv[kv].reshape(NALL * SLOTS * GP, COLS)).astype(BF16)
+            side = [side_by_side(held1, pos * 2, 2) for pos in range(PREV + 1)] + [entry(1, kv)]
             cache_out[kv] = dot(turn, jnp.concatenate(side, axis=0)).astype(BF16)
 
     with jax.named_scope("self_out"):
@@ -527,7 +529,7 @@
         late[0].wait_recv()
         prod[:, :COLS] = dot(rows, wso[...])
         prod[:, COLS:] = dot(rows, far_wso[...])
-        head_sums(0, core_s, core_r, ys, yr, delta, cache_start)
+        head_sums(0, core_s, core_r, ys, yr, delta, lambda: cache_start(0))
 
     with jax.named_scope("cross_query_products"):
         states = hid[...]
@@ -602,17 +604,18 @@
         mixed[0] = (acc / whole).astype(BF16)
 
     with jax.named_scope("cross_out"):
-        rows = gather_rows(2, mixed, cache_end)
+        rows = gather_rows(2, mixed)
         inward[4].wait()
         late[3].wait_recv()
         prod[:, :COLS] = dot(rows, wco[...])
         prod[:, COLS:] = dot(rows, far_wco[...])
-        head_sums(1, core_s2, core_r2, ys2, yr2, delta2)
+        head_sums(1, core_s2, core_r2, ys2, yr2, delta2, lambda: cache_start(1))
 
     with jax.named_scope("pair_columns"):
         last_s[...] = summed[:, COLS:].astype(BF16)
         copy = pair_copy(9, last_s, last_r, pair_peer)
         begin(copy)
+        cache_end()
         for dz in range(NZ):
             for t in range(2):
                 rows = slice(dz * BLK + t * RB, dz * BLK + (t + 1) * RB)
@@ -665,14 +668,15 @@
             *[pltpu.VMEM((NZ - 1, BLK, wide2), BF16)] * 2,
             pltpu.VMEM((ROWS, wide2), F32),
             *[pltpu.VMEM((NZ - 1, BLK, wide2), BF16)] * 2,
-            *[pltpu.VMEM((2, NALL, SLOTS * CP, COLS), BF16)] * 2,
-            *[pltpu.VMEM((NALL, SLOTS * KP, LANES), BF16)] * 6,
+            *[pltpu.VMEM((NALL, SLOTS * CP, COLS), BF16)] * 2,
+            *[pltpu.VMEM((2, NALL, SLOTS * GP, COLS), BF16)] * 2,
+            *[pltpu.VMEM((NALL, SLOTS * KP, LANES), BF16)] * 4,
             *[pltpu.VMEM((NZ, BLK, INNER), BF16)] * 3,
             *[pltpu.VMEM((ROWS, COLS), BF16)] * 2,
             *head_buffers,
             *head_buffers,
             dma((10,)), dma((10,)), dma((3, NZ - 1)), dma((3, NZ - 1)),
-            dma((2, NALL)), dma((2, NALL)), dma((NALL,)), dma((NALL,)),
+            dma((NALL,)), dma((NALL,)), dma((2, NALL)), dma((2, NALL)),
             dma((3, NZ)), dma((3, NZ)),
             dma((2,)), dma((2,)), dma((2, NY - 1)), dma((2, NY - 1)),
             dma((2, NY)), dma((2, NY)), dma((2, NY)), dma((2, NY)),

time: 156 us -> 149 us (0.955)
  Pallas kernels: 153 us -> 145 us
    pallas_call x1, Pallas kernels: 153 us -> 145 us  [body(): pl.pallas_call(kernel, out_shape=(jax.ShapeDtypeStruct(hidden_in.shape, F...]
where the time goes in v4:
time: 149 us; the launch traced here: 148 us
  Pallas kernels  145 us (97%)
  other arithmetic  1.94 us (1%)
    pallas_call x1, Pallas kernels, body(): pl.pallas_call(kernel, out_shape=(jax.ShapeDtypeStruct(hidden_in.shape, F...  145 us

profile of v4, /device:TPU:1, one launch (start us, length us, event | category | flops | bytes accessed | tf_op | source)
XLA Modules:
  0.0 148.3 jit_solution(8997546833315966228)
XLA Ops:
  0.6 0.0 copy-start
  0.6 145.0 %decode.1 = (f32[2,256,256]{2,1,0:T(8,128)}, bf16[2,128,512]{2,1,0:T(8,128)(2,1)}) custom-call(f32[2,256,256]{2,1,0:T(8,128)} %hidden.1, f32[2,256]{1,0:T(2,128)} %gains.1, bf16[3,256,512]{2,1,0:T(8,128)(2,1)} %bitcast.7, bf16[512,256]{1,0:T(8,128)(2,1)} %wso_hbm.1, bf16[256,512]{1,0:T(8,128)(2,1)} %wcq_hbm.1, bf16[512,256]{1,0:T(8,128)(2,1)} %wco_hbm.1, ...), custom_call_target="tpu_custom_call" | custom-call | tf_op jit(solution)/shard_map/decode/pallas_call | solution.py:642
  145.6 0.0 copy-done
  145.6 0.0 copy-start.1
  145.6 1.9 %add.3 = f32[2,256,256]{2,1,0:T(8,128)} add(f32[2,256,256]{2,1,0:T(8,128)S(1)} %copy-done, f32[2,256,256]{2,1,0:T(8,128)} %get-tuple-element.4) | non-fusion elementwise | flops 131072 | bytes 1572864 | tf_op jit(solution)/shard_map/add | solution.py:693
  147.6 0.0 copy-done.1
  147.6 0.7 copy.14
Async XLA Ops:
  0.6 145.0 %copy-start = (f32[2,256,256]{2,1,0:T(8,128)S(1)}, f32[2,256,256]{2,1,0:T(8,128)}, u32[]{:S(2)}) copy-start(f32[2,256,256]{2,1,0:T(8,128)} %hidden.1) | copy-start | bytes 1572868
  145.6 2.0 %copy-start.1 = (bf16[2,128,512]{2,1,0:T(8,128)(2,1)S(1)}, bf16[2,128,512]{2,1,0:T(8,128)(2,1)}, u32[]{:S(2)}) copy-start(bf16[2,128,512]{2,1,0:T(8,128)(2,1)} %get-tuple-element.5) | copy-start | bytes 786436

commit v5 on v4

--- a/solution.py
+++ b/solution.py
@@ -16,6 +16,7 @@
 BLK = 2 * RB
 ROWS = NZ * BLK
 HALF = ROWS // 2
+STREAM = ROWS // 2
 INNER = 512
 COLS = 256
 WIDE = 2 * COLS
@@ -282,102 +283,94 @@
         for copy in late:
             begin(copy)
 
-    def scatter_sums(phase, width, zs, zr, own, meanwhile=None):
+    def scatter_start(i, width, size, zs, zr, own):
         for dz in far_first:
-            rows = slice(dz * BLK, (dz + 1) * BLK)
+            rows = slice(dz * size, (dz + 1) * size)
             zs[dz - 1, :, :width] = own[rows, :width].astype(BF16)
             zs[dz - 1, :, width:] = encode(own[rows, width:])
-            begin(z_copy(phase, zs, zr, dz))
-        if meanwhile:
-            meanwhile()
-        total, squares = own[:BLK, :width], own[:BLK, width:]
+            begin(z_copy(i, zs, zr, dz))
+
+    def scatter_end(i, width, size, zs, zr, own):
+        total, squares = own[:size, :width], own[:size, width:]
         for dz in far_first[::-1]:
-            z_copy(phase, zs, zr, dz).wait_recv()
+            z_copy(i, zs, zr, dz).wait_recv()
             arrived = zr[dz - 1]
             total += arrived[:, :width].astype(F32)
             squares += dot(arrived[:, width:], decode_row())
         return total, lax.rsqrt(squares[:, :1] / D + EPS)
 
     def square_sums(states):
-        return jnp.broadcast_to(jnp.sum(states * states, axis=1, keepdims=True), (ROWS, LANES))
-
-    def gather_rows(phase, blocks, meanwhile=None):
-        def copy(dz):
+        return jnp.broadcast_to(jnp.sum(states * states, axis=1, keepdims=True), (states.shape[0], LANES))
+
+    def gather_start(i, blocks):
+        for dz in far_first:
             back = NZ - dz
-            return remote(
-                blocks.at[0], blocks.at[back], sem_gs.at[phase, dz], sem_gr.at[phase, back], z_peer(dz)
-            )
-
-        for dz in far_first:
-            begin(copy(dz))
-        if meanwhile:
-            meanwhile()
+            begin(remote(blocks.at[0], blocks.at[back], sem_gs.at[i, dz], sem_gr.at[i, back], z_peer(dz)))
+
+    def gather_end(i, blocks):
         for dz in far_first[::-1]:
-            remote(
-                blocks.at[0], blocks.at[dz], sem_gs.at[phase, dz], sem_gr.at[phase, dz], z_peer(dz)
-            ).wait_recv()
-        return blocks[...].reshape(ROWS, INNER)
-
-    quarter = HALF // NY
+            remote(blocks.at[0], blocks.at[dz], sem_gs.at[i, dz], sem_gr.at[i, dz], z_peer(dz)).wait_recv()
+        return blocks[...].reshape(STREAM, INNER)
+
+    part_rows = STREAM // 2
+    quarter = part_rows // NY
+    order, nearest = (2, 1, 3), (1, 3, 2)
 
     def quarter_rows(half, dy):
-        start = half * HALF + lax.rem(y + dy, NY) * quarter
+        start = half * part_rows + lax.rem(y + dy, NY) * quarter
         return pl.ds(pl.multiple_of(start, quarter), quarter)
 
-    def head_sums(phase, core_s, core_r, ys, yr, delta, meanwhile=None):
-        core_s[...] = prod[its_half, :].astype(BF16)
-        copy = remote(core_s, core_r, sem_cs.at[phase], sem_cr.at[phase], core_peer)
+    def half_rows(half):
+        return pl.ds(pl.multiple_of(half * part_rows, part_rows), part_rows)
+
+    def head_sums(i, first, product, total_out, core_s, core_r, ys, yr, delta, meanwhile):
+        core_s[...] = product[half_rows(1 - core), :].astype(BF16)
+        copy = remote(core_s, core_r, sem_cs.at[i], sem_cr.at[i], core_peer)
         begin(copy)
+        yield
         copy.wait_recv()
-        prod[my_half, :] += core_r[...].astype(F32)
+        product[half_rows(core), :] += core_r[...].astype(F32)
 
         def copy_sum(dy):
             return remote(
-                ys.at[dy - 1], yr.at[dy - 1], sem_ys.at[phase, dy - 1], sem_yr.at[phase, dy - 1], y_peer(dy)
+                ys.at[dy - 1], yr.at[dy - 1], sem_ys.at[i, dy - 1], sem_yr.at[i, dy - 1], y_peer(dy)
             )
 
-        order = (2, 1, 3)
         for dy in order:
-            ys[dy - 1] = prod[quarter_rows(core, dy), :].astype(BF16)
+            ys[dy - 1] = product[quarter_rows(core, dy), :].astype(BF16)
             begin(copy_sum(dy))
-        if meanwhile:
-            meanwhile()
-        total = prod[quarter_rows(core, 0), :]
-        for dy in (1, 3, 2):
+        meanwhile()
+        yield
+        total = product[quarter_rows(core, 0), :]
+        for dy in nearest:
             copy_sum(dy).wait_recv()
             total += yr[dy - 1].astype(F32)
         delta[0, 0] = total.astype(BF16)
 
-        def copy_y(dy):
+        def copy_c(dy):
+            return remote(delta.at[0, dy], delta.at[1, dy], sem_es.at[i, dy], sem_er.at[i, dy], core_peer)
+
+        for dy in order:
             back = NY - dy
-            return remote(
-                delta.at[0, 0], delta.at[0, back], sem_ds.at[phase, dy], sem_dr.at[phase, back], y_peer(dy)
-            )
-
-        def copy_c(dy):
-            return remote(
-                delta.at[0, dy], delta.at[1, dy], sem_es.at[phase, dy], sem_er.at[phase, dy], core_peer
-            )
-
-        for dy in order:
-            begin(copy_y(dy))
+            begin(remote(delta.at[0, 0], delta.at[0, back], sem_ds.at[i, dy], sem_dr.at[i, back], y_peer(dy)))
         begin(copy_c(0))
-        for dy in (1, 3, 2):
+        yield
+        for dy in nearest:
             remote(
-                delta.at[0, 0], delta.at[0, dy], sem_ds.at[phase, dy], sem_dr.at[phase, dy], y_peer(dy)
+                delta.at[0, 0], delta.at[0, dy], sem_ds.at[i, dy], sem_dr.at[i, dy], y_peer(dy)
             ).wait_recv()
             begin(copy_c(dy))
+        yield
         for dy in range(NY):
             copy_c(dy).wait_recv()
         for part in range(2):
             half = core if part == 0 else 1 - core
             for dy in range(NY):
                 added = delta[part, dy].astype(F32)
-                if phase == 0:
-                    hid[quarter_rows(half, dy), :] += added
-                    summed[quarter_rows(half, dy), :] = added
+                if first:
+                    total_out[quarter_rows(half, dy), :] = added
                 else:
-                    summed[quarter_rows(half, dy), :] += added
+                    total_out[quarter_rows(half, dy), :] += added
 
     with jax.named_scope("qkv_products"):
         width1 = 3 * INNER
@@ -402,159 +395,18 @@
             own1[:, j * INNER : (j + 1) * INNER] += dot(normed, far_wqkv[j])
 
     with jax.named_scope("qkv_sums"):
-        total, scale = scatter_sums(0, width1, zs1, zr1, own1, late_start)
+        scatter_start(0, width1, BLK, zs1, zr1, own1)
+        late_start()
+        total, scale = scatter_end(0, width1, BLK, zs1, zr1, own1)
         qkv = (total * scale).astype(BF16)
 
-    def ask_copy(o):
-        return remote(ask_send.at[o], ask_recv.at[o], sem_as.at[o], sem_ar.at[o], back_peer(o))
-
-    def reply_copy(o):
-        return remote(reply_send.at[o], reply_recv.at[o], sem_rs.at[o], sem_rr.at[o], all_peer(o))
-
-    def grown_copy(kv, o):
-        return remote(
-            grown_send.at[kv, o], grown_recv.at[kv, o], sem_ks.at[kv, o], sem_kr.at[kv, o], all_peer(o)
-        )
-
-    def side_by_side(rows, first, count):
-        return jnp.concatenate([rows[(first + p) * RB : (first + p + 1) * RB] for p in range(count)], axis=1)
-
-    def stacked(rows):
-        return [rows[:, p * LANES : (p + 1) * LANES] for p in range(rows.shape[1] // LANES)]
-
-    def entry(t, kv):
-        return qkv[t * RB : (t + 1) * RB, (1 + kv) * INNER : (2 + kv) * INNER]
-
-    messages = (NALL, SLOTS * KP, LANES)
-    flat = (NALL * SLOTS * KP, LANES)
-    queries_of = [
-        (qkv[t * RB : (t + 1) * RB, :INNER].astype(F32) * 0.125).astype(BF16) for t in range(2)
-    ]
-    with jax.named_scope("query_send"):
-        send1, recv1 = picks(parents[1:2, :], x, z, beam)
-        four = stacked(queries_of[1])
-        asked = jnp.concatenate(four + four, axis=0)
-        ask_send[...] = dot(spread_matrix(recv1, KP), asked).astype(BF16).reshape(messages)
-        ask_recv[0] = ask_send[0]
-        for o in range(1, NALL):
-            begin(ask_copy(o))
-
-    with jax.named_scope("parent_attention"):
-        same_head = (iota((INNER, INNER), 0) >> 6) == (iota((INNER, INNER), 1) >> 6)
-        ones = jnp.where(same_head, 1.0, 0.0).astype(BF16)
-        of_head = jnp.where((iota((8, INNER), 1) >> 6) == iota((8, INNER), 0), 1.0, 0.0).astype(BF16)
-        wide_bias = sum(
-            lax.dot_general(part.astype(BF16), of_head, (((0,), (0,)), ((), ())), preferred_element_type=F32)
-            for part in split3(bias[...])
-        )
-        pick = gather_matrix(recv0, CP)
-        for o in range(1, NALL):
-            hop_copy(o).wait_recv()
-        held0 = dot(pick, hop_recv[...].reshape(NALL * SLOTS * CP, COLS)).astype(BF16)
-        grown0 = [
-            [side_by_side(held0, (kv * PREV + pos) * 2, 2) for pos in range(PREV)] + [entry(0, kv)] for kv in range(2)
-        ]
-        copies = [[dot(send1, rows) for rows in side] for side in grown0]
-        rows_of_piece = [piece_rows(p) for p in range(5)]
-        back = jnp.concatenate(rows_of_piece, axis=0)
-        for o in range(1, NALL):
-            ask_copy(o).wait_recv()
-        arrived = ask_recv[...].reshape(flat)
-        q = jnp.concatenate([dot(rows_of_piece[p], arrived) for p in range(4)], axis=1)
-        last = PREV + 1
-        acc, peak, whole = attend(
-            q, *copies, [wide_bias[last - j : last - j + 1, :] for j in range(last)], ones
-        )
-        mine = (acc / whole).astype(BF16)
-        lse = peak + jnp.log(whole)
-        code = head_codes(stacked(lse))
-        turned = lax.dot_general(
-            back, jnp.concatenate(stacked(mine) + [code], axis=0), (((0,), (0,)), ((), ())), preferred_element_type=F32
-        )
-        reply_send[...] = turned.astype(BF16).reshape(messages)
-        reply_recv[0] = reply_send[0]
-        for o in range(1, NALL):
-            begin(reply_copy(o))
-
-    with jax.named_scope("self_attention"):
-        acc, _, whole = attend(
-            queries_of[0].astype(F32), *grown0,
-            [wide_bias[PREV - j : PREV - j + 1, :] for j in range(PREV + 1)], ones,
-        )
-        att[0, :RB, :] = (acc / whole).astype(BF16)
-        pick1 = gather_matrix(recv1, KP)
-        spread_heads = decode_heads()
-        fresh = queries_of[1].astype(F32) * entry(1, 0).astype(F32)
-        high = fresh.astype(BF16)
-        low = (fresh - high.astype(F32)).astype(BF16)
-        score = dot(high, ones) + dot(low, ones) + wide_bias[0:1, :]
-        for o in range(1, NALL):
-            reply_copy(o).wait_recv()
-        replies = dot(pick1, reply_recv[...].reshape(flat)).astype(BF16)
-        lse = dot(replies[4 * RB : 5 * RB], spread_heads)
-        peak = jnp.maximum(lse, score)
-        w_old, w_new = jnp.exp(lse - peak), jnp.exp(score - peak)
-        acc = side_by_side(replies, 0, 4).astype(F32) * w_old + w_new * entry(1, 1).astype(F32)
-        att[0, RB:, :] = (acc / (w_old + w_new)).astype(BF16)
-
-    def cache_ready():
-        spread = spread_matrix(send1, GP)
-        for kv in range(2):
-            new = entry(0, kv)
-            halves = [new[:, :COLS], new[:, COLS:]]
-            first = kv * PREV * 2 * RB
-            rows = jnp.concatenate([held0[first : first + PREV * 2 * RB], *halves, *halves], axis=0)
-            grown_send[kv] = dot(spread, rows).astype(BF16).reshape(NALL, SLOTS * GP, COLS)
-            grown_recv[kv, 0] = grown_send[kv, 0]
-
-    def cache_start(kv):
-        for o in range(1, NALL):
-            begin(grown_copy(kv, o))
-
-    def cache_end():
-        pick = gather_matrix(recv1, GP)
-        place = iota((RB * (PREV + 2), RB * (PREV + 2)), 0)
-        from_row = (place & 7) * RB + (place >> 3)
-        turn = jnp.where(from_row == iota(place.shape, 1), 1.0, 0.0).astype(BF16)
-        for kv in range(2):
-            for o in range(1, NALL):
-                grown_copy(kv, o).wait_recv()
-            held1 = dot(pick, grown_recv[kv].reshape(NALL * SLOTS * GP, COLS)).astype(BF16)
-            side = [side_by_side(held1, pos * 2, 2) for pos in range(PREV + 1)] + [entry(1, kv)]
-            cache_out[kv] = dot(turn, jnp.concatenate(side, axis=0)).astype(BF16)
-
-    with jax.named_scope("self_out"):
-        rows = gather_rows(0, att, cache_ready)
-        inward[1].wait()
-        late[0].wait_recv()
-        prod[:, :COLS] = dot(rows, wso[...])
-        prod[:, COLS:] = dot(rows, far_wso[...])
-        head_sums(0, core_s, core_r, ys, yr, delta, lambda: cache_start(0))
-
-    with jax.named_scope("cross_query_products"):
-        states = hid[...]
-        gain = jnp.concatenate([gains[1:2, :], near_gain[1:2, :]], axis=1)
-        normed = (states * gain).astype(BF16)
-        inward[2].wait()
-        late[1].wait_recv()
-        own2[:, :INNER] = dot(normed[:, :COLS], wcq[...]) + dot(normed[:, COLS:], far_wcq[...])
-        own2[:, INNER:] = square_sums(states)
-
-    with jax.named_scope("cross_query_sums"):
-        total, scale = scatter_sums(1, INNER, zs2, zr2, own2)
-        query[0] = ((total * scale).astype(BF16).astype(F32) * 0.125).astype(BF16)
-
-    with jax.named_scope("cross_query_gather"):
-        queries = gather_rows(1, query)
-
-    with jax.named_scope("cross_partial"):
-        inward[3].wait()
-        late[2].wait_recv()
-        tokens = 2 * memory.shape[1]
+    spread_heads = decode_heads()
+    tokens = 2 * memory.shape[1]
+    pairs = []
+
+    def token_pairs():
         low_lane = iota((tokens, LANES), 1) < 64
-        low_out = iota((ROWS, LANES), 1) < 64
         one = jnp.where(low_lane, 1.0, 0.0)
-        accs, lses = [], []
         for p in range(INNER // LANES):
             cols = slice(p * LANES, (p + 1) * LANES)
             k, v = (
@@ -569,31 +421,75 @@
                 ],
                 axis=0,
             )
-            scores = dot_t(queries[:, cols], k2.astype(BF16))
+            pairs.append((k2.astype(BF16), v2.astype(BF16)))
+
+    def pair_columns(t):
+        return pair_copy(9 + t, last_s.at[t], last_r.at[t], pair_peer)
+
+    def stream(t):
+        gather_start(t, att.at[t])
+        yield
+        rows = gather_end(t, att.at[t])
+        if t == 0:
+            inward[1].wait()
+            late[0].wait_recv()
+        prod[t, :, :COLS] = dot(rows, wso[...])
+        prod[t, :, COLS:] = dot(rows, far_wso[...])
+        yield from head_sums(
+            t, True, prod.at[t], summed.at[t], core_s.at[t], core_r.at[t], ys.at[t], yr.at[t], delta.at[t],
+            lambda: cache_start(0) if t else None,
+        )
+
+        states = summed[t] + jnp.concatenate(
+            [hid[dz * BLK + t * RB : dz * BLK + (t + 1) * RB, :] for dz in range(NZ)], axis=0
+        )
+        gain = jnp.concatenate([gains[1:2, :], near_gain[1:2, :]], axis=1)
+        normed = (states * gain).astype(BF16)
+        if t == 0:
+            inward[2].wait()
+            late[1].wait_recv()
+        own = own2.at[t]
+        own[:, :INNER] = dot(normed[:, :COLS], wcq[...]) + dot(normed[:, COLS:], far_wcq[...])
+        own[:, INNER:] = square_sums(states)
+        scatter_start(1 + t, INNER, RB, zs2.at[t], zr2.at[t], own)
+        if t == 0:
+            inward[3].wait()
+            late[2].wait_recv()
+            token_pairs()
+        yield
+        total, scale = scatter_end(1 + t, INNER, RB, zs2.at[t], zr2.at[t], own)
+        query[t, 0] = ((total * scale).astype(BF16).astype(F32) * 0.125).astype(BF16)
+        gather_start(2 + t, query.at[t])
+        yield
+        queries = gather_end(2 + t, query.at[t])
+        low_out = iota((STREAM, LANES), 1) < 64
+        accs, lses = [], []
+        for p, (k2, v2) in enumerate(pairs):
+            cols = slice(p * LANES, (p + 1) * LANES)
+            scores = dot_t(queries[:, cols], k2)
             peak0 = jnp.max(scores[:, :tokens], axis=1, keepdims=True)
             peak1 = jnp.max(scores[:, tokens:], axis=1, keepdims=True)
             weights = jnp.concatenate(
                 [jnp.exp(scores[:, :tokens] - peak0), jnp.exp(scores[:, tokens:] - peak1)], axis=1
             )
-            both = dot(weights.astype(BF16), v2.astype(BF16))
+            both = dot(weights.astype(BF16), v2)
             lses.append(jnp.where(low_out, peak0, peak1) + jnp.log(both[:, LANES:]))
             acc = both[:, :LANES] / both[:, LANES:]
-            accs.append(acc[:BLK])
+            accs.append(acc[:RB])
             narrow = acc.astype(BF16)
             for dz in range(1, NZ):
-                zs3[dz - 1, :, cols] = narrow[dz * BLK : (dz + 1) * BLK]
+                zs3[t, dz - 1, :, cols] = narrow[dz * RB : (dz + 1) * RB]
         code = head_codes(lses)
         for dz in range(1, NZ):
-            zs3[dz - 1, :, INNER:] = code[dz * BLK : (dz + 1) * BLK]
-
-    with jax.named_scope("cross_join"):
+            zs3[t, dz - 1, :, INNER:] = code[dz * RB : (dz + 1) * RB]
         for dz in far_first:
-            begin(z_copy(2, zs3, zr3, dz))
-        peak = jnp.concatenate([lse[:BLK] for lse in lses], axis=1)
+            begin(z_copy(3 + t, zs3.at[t], zr3.at[t], dz))
+        yield
+        peak = jnp.concatenate([lse[:RB] for lse in lses], axis=1)
         parts = [(jnp.concatenate(accs, axis=1), peak)]
         for dz in far_first[::-1]:
-            z_copy(2, zs3, zr3, dz).wait_recv()
-            arrived = zr3[dz - 1]
+            z_copy(3 + t, zs3.at[t], zr3.at[t], dz).wait_recv()
+            arrived = zr3[t, dz - 1]
             parts.append((arrived[:, :INNER].astype(F32), dot(arrived[:, INNER:], spread_heads)))
             peak = jnp.maximum(peak, parts[-1][1])
         weights = [jnp.exp(lse - peak) for _, lse in parts]
@@ -601,30 +497,157 @@
         for (a, _), w in zip(parts[1:], weights[1:]):
             acc += a * w
             whole += w
-        mixed[0] = (acc / whole).astype(BF16)
-
-    with jax.named_scope("cross_out"):
-        rows = gather_rows(2, mixed)
-        inward[4].wait()
-        late[3].wait_recv()
-        prod[:, :COLS] = dot(rows, wco[...])
-        prod[:, COLS:] = dot(rows, far_wco[...])
-        head_sums(1, core_s2, core_r2, ys2, yr2, delta2, lambda: cache_start(1))
-
-    with jax.named_scope("pair_columns"):
-        last_s[...] = summed[:, COLS:].astype(BF16)
-        copy = pair_copy(9, last_s, last_r, pair_peer)
-        begin(copy)
-        cache_end()
+        mixed[t, 0] = (acc / whole).astype(BF16)
+        gather_start(4 + t, mixed.at[t])
+        yield
+        rows = gather_end(4 + t, mixed.at[t])
+        if t == 0:
+            inward[4].wait()
+            late[3].wait_recv()
+        prod[t, :, :COLS] = dot(rows, wco[...])
+        prod[t, :, COLS:] = dot(rows, far_wco[...])
+        yield from head_sums(
+            2 + t, False, prod.at[t], summed.at[t], core_s2.at[t], core_r2.at[t], ys2.at[t], yr2.at[t], delta2.at[t],
+            lambda: cache_start(1) if t else None,
+        )
+
+        last_s[t] = summed[t, :, COLS:].astype(BF16)
+        begin(pair_columns(t))
         for dz in range(NZ):
-            for t in range(2):
-                rows = slice(dz * BLK + t * RB, dz * BLK + (t + 1) * RB)
-                out[t, rows_at(0, dz), :] = summed[rows, :COLS]
-        copy.wait_recv()
+            out[t, rows_at(0, dz), :] = summed[t, dz * RB : (dz + 1) * RB, :COLS]
+
+    streams = [stream(t) for t in range(2)]
+
+    def ask_copy(o):
+        return remote(ask_send.at[o], ask_recv.at[o], sem_as.at[o], sem_ar.at[o], back_peer(o))
+
+    def reply_copy(o):
+        return remote(reply_send.at[o], reply_recv.at[o], sem_rs.at[o], sem_rr.at[o], all_peer(o))
+
+    def grown_copy(kv, o):
+        return remote(
+            grown_send.at[kv, o], grown_recv.at[kv, o], sem_ks.at[kv, o], sem_kr.at[kv, o], all_peer(o)
+        )
+
+    def side_by_side(rows, first, count):
+        return jnp.concatenate([rows[(first + p) * RB : (first + p + 1) * RB] for p in range(count)], axis=1)
+
+    def stacked(rows):
+        return [rows[:, p * LANES : (p + 1) * LANES] for p in range(rows.shape[1] // LANES)]
+
+    def entry(t, kv):
+        return qkv[t * RB : (t + 1) * RB, (1 + kv) * INNER : (2 + kv) * INNER]
+
+    messages = (NALL, SLOTS * KP, LANES)
+    flat = (NALL * SLOTS * KP, LANES)
+    queries_of = [
+        (qkv[t * RB : (t + 1) * RB, :INNER].astype(F32) * 0.125).astype(BF16) for t in range(2)
+    ]
+    with jax.named_scope("query_send"):
+        send1, recv1 = picks(parents[1:2, :], x, z, beam)
+        four = stacked(queries_of[1])
+        asked = jnp.concatenate(four + four, axis=0)
+        ask_send[...] = dot(spread_matrix(recv1, KP), asked).astype(BF16).reshape(messages)
+        ask_recv[0] = ask_send[0]
+        for o in range(1, NALL):
+            begin(ask_copy(o))
+
+    with jax.named_scope("parent_attention"):
+        same_head = (iota((INNER, INNER), 0) >> 6) == (iota((INNER, INNER), 1) >> 6)
+        ones = jnp.where(same_head, 1.0, 0.0).astype(BF16)
+        of_head = jnp.where((iota((8, INNER), 1) >> 6) == iota((8, INNER), 0), 1.0, 0.0).astype(BF16)
+        wide_bias = sum(
+            lax.dot_general(part.astype(BF16), of_head, (((0,), (0,)), ((), ())), preferred_element_type=F32)
+            for part in split3(bias[...])
+        )
+        pick = gather_matrix(recv0, CP)
+        for o in range(1, NALL):
+            hop_copy(o).wait_recv()
+        held0 = dot(pick, hop_recv[...].reshape(NALL * SLOTS * CP, COLS)).astype(BF16)
+        grown0 = [
+            [side_by_side(held0, (kv * PREV + pos) * 2, 2) for pos in range(PREV)] + [entry(0, kv)] for kv in range(2)
+        ]
+        acc, _, whole = attend(
+            queries_of[0].astype(F32), *grown0,
+            [wide_bias[PREV - j : PREV - j + 1, :] for j in range(PREV + 1)], ones,
+        )
+        att[0, 0] = (acc / whole).astype(BF16)
+        next(streams[0])
+        copies = [[dot(send1, rows) for rows in side] for side in grown0]
+        rows_of_piece = [piece_rows(p) for p in range(5)]
+        back = jnp.concatenate(rows_of_piece, axis=0)
+        for o in range(1, NALL):
+            ask_copy(o).wait_recv()
+        arrived = ask_recv[...].reshape(flat)
+        q = jnp.concatenate([dot(rows_of_piece[p], arrived) for p in range(4)], axis=1)
+        last = PREV + 1
+        acc, peak, whole = attend(
+            q, *copies, [wide_bias[last - j : last - j + 1, :] for j in range(last)], ones
+        )
+        mine = (acc / whole).astype(BF16)
+        lse = peak + jnp.log(whole)
+        code = head_codes(stacked(lse))
+        turned = lax.dot_general(
+            back, jnp.concatenate(stacked(mine) + [code], axis=0), (((0,), (0,)), ((), ())), preferred_element_type=F32
+        )
+        reply_send[...] = turned.astype(BF16).reshape(messages)
+        reply_recv[0] = reply_send[0]
+        for o in range(1, NALL):
+            begin(reply_copy(o))
+
+    with jax.named_scope("self_attention"):
+        pick1 = gather_matrix(recv1, KP)
+        next(streams[0])
+        fresh = queries_of[1].astype(F32) * entry(1, 0).astype(F32)
+        high = fresh.astype(BF16)
+        low = (fresh - high.astype(F32)).astype(BF16)
+        score = dot(high, ones) + dot(low, ones) + wide_bias[0:1, :]
+        next(streams[0])
+        for o in range(1, NALL):
+            reply_copy(o).wait_recv()
+        replies = dot(pick1, reply_recv[...].reshape(flat)).astype(BF16)
+        lse = dot(replies[4 * RB : 5 * RB], spread_heads)
+        peak = jnp.maximum(lse, score)
+        w_old, w_new = jnp.exp(lse - peak), jnp.exp(score - peak)
+        acc = side_by_side(replies, 0, 4).astype(F32) * w_old + w_new * entry(1, 1).astype(F32)
+        att[1, 0] = (acc / (w_old + w_new)).astype(BF16)
+        next(streams[1])
+
+    def cache_ready():
+        spread = spread_matrix(send1, GP)
+        for kv in range(2):
+            new = entry(0, kv)
+            halves = [new[:, :COLS], new[:, COLS:]]
+            first = kv * PREV * 2 * RB
+            rows = jnp.concatenate([held0[first : first + PREV * 2 * RB], *halves, *halves], axis=0)
+            grown_send[kv] = dot(spread, rows).astype(BF16).reshape(NALL, SLOTS * GP, COLS)
+            grown_recv[kv, 0] = grown_send[kv, 0]
+
+    def cache_start(kv):
+        for o in range(1, NALL):
+            begin(grown_copy(kv, o))
+
+    def cache_end():
+        pick = gather_matrix(recv1, GP)
+        place = iota((RB * (PREV + 2), RB * (PREV + 2)), 0)
+        from_row = (place & 7) * RB + (place >> 3)
+        turn = jnp.where(from_row == iota(place.shape, 1), 1.0, 0.0).astype(BF16)
+        for kv in range(2):
+            for o in range(1, NALL):
+                grown_copy(kv, o).wait_recv()
+            held1 = dot(pick, grown_recv[kv].reshape(NALL * SLOTS * GP, COLS)).astype(BF16)
+            side = [side_by_side(held1, pos * 2, 2) for pos in range(PREV + 1)] + [entry(1, kv)]
+            cache_out[kv] = dot(turn, jnp.concatenate(side, axis=0)).astype(BF16)
+
+    cache_ready()
+    running = list(streams)
+    while running:
+        running = [stream for stream in running if next(stream, "end") != "end"]
+    cache_end()
+    for t in range(2):
+        pair_columns(t).wait_recv()
         for dz in range(NZ):
-            for t in range(2):
-                rows = slice(dz * BLK + t * RB, dz * BLK + (t + 1) * RB)
-                out[t, rows_at(1, dz), :] = last_r[rows, :].astype(F32)
+            out[t, rows_at(1, dz), :] = last_r[t, dz * RB : (dz + 1) * RB, :].astype(F32)
     for copy in pending:
         copy.wait_send()
 
@@ -634,9 +657,10 @@
 ):
     dma = pltpu.SemaphoreType.DMA
     wide1, wide2 = 3 * INNER + LANES, INNER + LANES
-    half_pair = [pltpu.VMEM((HALF, WIDE), BF16)] * 2
-    quarters = [pltpu.VMEM((NY - 1, HALF // NY, WIDE), BF16)] * 2
-    head_buffers = [*half_pair, *quarters, pltpu.VMEM((2, NY, HALF // NY, WIDE), BF16)]
+    part = STREAM // 2
+    half_pair = [pltpu.VMEM((2, part, WIDE), BF16)] * 2
+    quarters = [pltpu.VMEM((2, NY - 1, part // NY, WIDE), BF16)] * 2
+    head_buffers = [*half_pair, *quarters, pltpu.VMEM((2, 2, NY, part // NY, WIDE), BF16)]
     in_vmem = pl.BlockSpec(memory_space=pltpu.VMEM)
     in_hbm = pl.BlockSpec(memory_space=pl.ANY)
     added, cache_rows = pl.pallas_call(
@@ -662,24 +686,25 @@
             pltpu.VMEM(w_cross_q.shape, BF16),
             pltpu.VMEM(w_cross_out.shape, BF16),
             pltpu.VMEM(memory.shape, BF16),
-            *[pltpu.VMEM((ROWS, WIDE), F32)] * 3,
+            pltpu.VMEM((ROWS, WIDE), F32),
+            *[pltpu.VMEM((2, STREAM, WIDE), F32)] * 2,
             *[pltpu.VMEM((NZ - 1, BLK, wide1), BF16)] * 2,
             pltpu.VMEM((ROWS, wide1), F32),
-            *[pltpu.VMEM((NZ - 1, BLK, wide2), BF16)] * 2,
-            pltpu.VMEM((ROWS, wide2), F32),
-            *[pltpu.VMEM((NZ - 1, BLK, wide2), BF16)] * 2,
+            *[pltpu.VMEM((2, NZ - 1, RB, wide2), BF16)] * 2,
+            pltpu.VMEM((2, STREAM, wide2), F32),
+            *[pltpu.VMEM((2, NZ - 1, RB, wide2), BF16)] * 2,
             *[pltpu.VMEM((NALL, SLOTS * CP, COLS), BF16)] * 2,
             *[pltpu.VMEM((2, NALL, SLOTS * GP, COLS), BF16)] * 2,
             *[pltpu.VMEM((NALL, SLOTS * KP, LANES), BF16)] * 4,
-            *[pltpu.VMEM((NZ, BLK, INNER), BF16)] * 3,
-            *[pltpu.VMEM((ROWS, COLS), BF16)] * 2,
+            *[pltpu.VMEM((2, NZ, RB, INNER), BF16)] * 3,
+            *[pltpu.VMEM((2, STREAM, COLS), BF16)] * 2,
             *head_buffers,
             *head_buffers,
-            dma((10,)), dma((10,)), dma((3, NZ - 1)), dma((3, NZ - 1)),
+            dma((11,)), dma((11,)), dma((5, NZ - 1)), dma((5, NZ - 1)),
             dma((NALL,)), dma((NALL,)), dma((2, NALL)), dma((2, NALL)),
-            dma((3, NZ)), dma((3, NZ)),
-            dma((2,)), dma((2,)), dma((2, NY - 1)), dma((2, NY - 1)),
-            dma((2, NY)), dma((2, NY)), dma((2, NY)), dma((2, NY)),
+            dma((6, NZ)), dma((6, NZ)),
+            dma((4,)), dma((4,)), dma((4, NY - 1)), dma((4, NY - 1)),
+            dma((4, NY)), dma((4, NY)), dma((4, NY)), dma((4, NY)),
             dma((NALL,)), dma((NALL,)), dma((NALL,)), dma((NALL,)), dma((5,)),
         ],
         compiler_params=pltpu.CompilerParams(

time: 149 us -> 152 us (1.020)
  Pallas kernels: 145 us -> 149 us
    pallas_call x1, Pallas kernels: 145 us -> 149 us  [body(): pl.pallas_call(kernel, out_shape=(jax.ShapeDtypeStruct(hidden_in.shape, F...]
where the time goes in v5:
time: 152 us
  Pallas kernels  149 us (98%)
  other arithmetic  1.94 us (1%)
    pallas_call x1, Pallas kernels, body(): pl.pallas_call(kernel, out_shape=(jax.ShapeDtypeStruct(hidden_in.shape, F...  149 us

profile of v5, /device:TPU:1, one launch (start us, length us, event | category | flops | bytes accessed | tf_op | source)
XLA Modules:
  0.0 151.9 jit_solution(16640218046232014340)
XLA Ops:
  0.6 0.0 copy-start
  0.6 148.6 %decode.1 = (f32[2,256,256]{2,1,0:T(8,128)}, bf16[2,128,512]{2,1,0:T(8,128)(2,1)}) custom-call(f32[2,256,256]{2,1,0:T(8,128)} %hidden.1, f32[2,256]{1,0:T(2,128)} %gains.1, bf16[3,256,512]{2,1,0:T(8,128)(2,1)} %bitcast.7, bf16[512,256]{1,0:T(8,128)(2,1)} %wso_hbm.1, bf16[256,512]{1,0:T(8,128)(2,1)} %wcq_hbm.1, bf16[512,256]{1,0:T(8,128)(2,1)} %wco_hbm.1, ...), custom_call_target="tpu_custom_call" | custom-call | tf_op jit(solution)/shard_map/decode/pallas_call | solution.py:666
  149.3 0.0 copy-done
  149.3 0.0 copy-start.1
  149.3 1.9 %add.3 = f32[2,256,256]{2,1,0:T(8,128)} add(f32[2,256,256]{2,1,0:T(8,128)S(1)} %copy-done, f32[2,256,256]{2,1,0:T(8,128)} %get-tuple-element.4) | non-fusion elementwise | flops 131072 | bytes 1572864 | tf_op jit(solution)/shard_map/add | solution.py:718
  151.2 0.0 copy-done.1
  151.2 0.7 copy.14
Async XLA Ops:
  0.6 148.6 %copy-start = (f32[2,256,256]{2,1,0:T(8,128)S(1)}, f32[2,256,256]{2,1,0:T(8,128)}, u32[]{:S(2)}) copy-start(f32[2,256,256]{2,1,0:T(8,128)} %hidden.1) | copy-start | bytes 1572868
  149.3 2.0 %copy-start.1 = (bf16[2,128,512]{2,1,0:T(8,128)(2,1)S(1)}, bf16[2,128,512]{2,1,0:T(8,128)(2,1)}, u32[]{:S(2)}) copy-start(bf16[2,128,512]{2,1,0:T(8,128)(2,1)} %get-tuple-element.5) | copy-start | bytes 786436

commit v6 on v4

--- a/solution.py
+++ b/solution.py
@@ -511,17 +511,20 @@
         for o in range(1, NALL):
             begin(grown_copy(kv, o))
 
-    def cache_end():
-        pick = gather_matrix(recv1, GP)
-        place = iota((RB * (PREV + 2), RB * (PREV + 2)), 0)
-        from_row = (place & 7) * RB + (place >> 3)
-        turn = jnp.where(from_row == iota(place.shape, 1), 1.0, 0.0).astype(BF16)
-        for kv in range(2):
-            for o in range(1, NALL):
-                grown_copy(kv, o).wait_recv()
-            held1 = dot(pick, grown_recv[kv].reshape(NALL * SLOTS * GP, COLS)).astype(BF16)
-            side = [side_by_side(held1, pos * 2, 2) for pos in range(PREV + 1)] + [entry(1, kv)]
-            cache_out[kv] = dot(turn, jnp.concatenate(side, axis=0)).astype(BF16)
+    arrange = []
+
+    def cache_end(kv):
+        if not arrange:
+            place = iota((RB * (PREV + 2), RB * (PREV + 2)), 0)
+            from_row = (place & 7) * RB + (place >> 3)
+            turn = jnp.where(from_row == iota(place.shape, 1), 1.0, 0.0).astype(BF16)
+            arrange.extend((gather_matrix(recv1, GP), turn))
+        pick, turn = arrange
+        for o in range(1, NALL):
+            grown_copy(kv, o).wait_recv()
+        held1 = dot(pick, grown_recv[kv].reshape(NALL * SLOTS * GP, COLS)).astype(BF16)
+        side = [side_by_side(held1, pos * 2, 2) for pos in range(PREV + 1)] + [entry(1, kv)]
+        cache_out[kv] = dot(turn, jnp.concatenate(side, axis=0)).astype(BF16)
 
     with jax.named_scope("self_out"):
         rows = gather_rows(0, att, cache_ready)
@@ -604,7 +607,7 @@
         mixed[0] = (acc / whole).astype(BF16)
 
     with jax.named_scope("cross_out"):
-        rows = gather_rows(2, mixed)
+        rows = gather_rows(2, mixed, lambda: cache_end(0))
         inward[4].wait()
         late[3].wait_recv()
         prod[:, :COLS] = dot(rows, wco[...])
@@ -615,7 +618,7 @@
         last_s[...] = summed[:, COLS:].astype(BF16)
         copy = pair_copy(9, last_s, last_r, pair_peer)
         begin(copy)
-        cache_end()
+        cache_end(1)
         for dz in range(NZ):
             for t in range(2):
                 rows = slice(dz * BLK + t * RB, dz * BLK + (t + 1) * RB)

time: 149 us -> 149 us (level)
  no operation moved by 1% of the time
where the time goes in v6:
time: 149 us; the launch traced here: 148 us
  Pallas kernels  145 us (97%)
  other arithmetic  1.94 us (1%)
    pallas_call x1, Pallas kernels, body(): pl.pallas_call(kernel, out_shape=(jax.ShapeDtypeStruct(hidden_in.shape, F...  145 us

profile of v6, /device:TPU:1, one launch (start us, length us, event | category | flops | bytes accessed | tf_op | source)
XLA Modules:
  0.0 148.0 jit_solution(14193769989777588478)
XLA Ops:
  0.6 0.0 copy-start
  0.6 144.7 %decode.1 = (f32[2,256,256]{2,1,0:T(8,128)}, bf16[2,128,512]{2,1,0:T(8,128)(2,1)}) custom-call(f32[2,256,256]{2,1,0:T(8,128)} %hidden.1, f32[2,256]{1,0:T(2,128)} %gains.1, bf16[3,256,512]{2,1,0:T(8,128)(2,1)} %bitcast.7, bf16[512,256]{1,0:T(8,128)(2,1)} %wso_hbm.1, bf16[256,512]{1,0:T(8,128)(2,1)} %wcq_hbm.1, bf16[512,256]{1,0:T(8,128)(2,1)} %wco_hbm.1, ...), custom_call_target="tpu_custom_call" | custom-call | tf_op jit(solution)/shard_map/decode/pallas_call | solution.py:645
  145.4 0.0 copy-done
  145.4 0.0 copy-start.1
  145.4 1.9 %add.3 = f32[2,256,256]{2,1,0:T(8,128)} add(f32[2,256,256]{2,1,0:T(8,128)S(1)} %copy-done, f32[2,256,256]{2,1,0:T(8,128)} %get-tuple-element.4) | non-fusion elementwise | flops 131072 | bytes 1572864 | tf_op jit(solution)/shard_map/add | solution.py:696
  147.3 0.0 copy-done.1
  147.3 0.7 copy.14
Async XLA Ops:
  0.6 144.7 %copy-start = (f32[2,256,256]{2,1,0:T(8,128)S(1)}, f32[2,256,256]{2,1,0:T(8,128)}, u32[]{:S(2)}) copy-start(f32[2,256,256]{2,1,0:T(8,128)} %hidden.1) | copy-start | bytes 1572868
  145.4 2.0 %copy-start.1 = (bf16[2,128,512]{2,1,0:T(8,128)(2,1)S(1)}, bf16[2,128,512]{2,1,0:T(8,128)(2,1)}, u32[]{:S(2)}) copy-start(bf16[2,128,512]{2,1,0:T(8,128)(2,1)} %get-tuple-element.5) | copy-start | bytes 786436
